TPU v7x, 128 devices: a whole 4x4x4 slice. The times are simulated.
128 devices in a mesh: dom: 128 (over x, y, z, core).
Axes of the slice: x: 4, y: 4, z: 4, core: 2. Of those that a mesh axis runs over, the one named last changes fastest.
Arguments:
- features: bfloat16 [262144, 256], P('dom'), may hold values from -24 to 24
- self_weight: bfloat16 [256, 256], replicated, may hold values from -0.375 to 0.375
- neighbour_weight: bfloat16 [256, 256], replicated, may hold values from -0.375 to 0.375
- send_lists: int32 [128, 128, 8], P('dom'), may hold values from 0 to 2047
- hub_nodes: int32 [128, 8], P('dom'), may hold values from 0 to 2047
- neighbours: int32 [262144, 16], P('dom'), may hold values from 0 to 4095
- counts: int32 [262144], P('dom'), may hold values from 1 to 16
- cotangent: bfloat16 [262144, 256], P('dom'), may hold values from -6 to 6
Outputs:
- activations: bfloat16 [262144, 256], P('dom')
- grad_features: float32 [262144, 256], P('dom')
- grad_weights: float32 [512, 256], P('dom')
All inputs are finite; a program needn't handle non-finite values.
Results may differ from a plain program's by a relative error of at most 0.0032.
Values may be sent and summed in bfloat16 or wider, within the bound.
No kernel may reach another device: no remote copies, remote signals or barrier semaphores. Data moves between devices by JAX's collectives and lax.ppermute only.
A program may use at most 64 MiB of HBM per device.

v0:
```python
import jax
import jax.numpy as jnp
from jax import lax
from jax.sharding import PartitionSpec as P


def slot_counts(index, usable, width):
    columns = jnp.arange(width, dtype=jnp.int32)
    hits = (index[:, :, None] == columns[None, None, :]) & usable[:, :, None]
    return jnp.sum(hits.astype(jnp.float32), axis=1)


def gather_sum(source_rows, index, usable):
    node_rows = index.shape[0]
    block_rows = min(512, node_rows)
    blocks = node_rows // block_rows
    index_blocks = index.reshape(blocks, block_rows, index.shape[1])
    usable_blocks = usable.reshape(blocks, block_rows, usable.shape[1])
    width = source_rows.shape[0]

    def gather_one_block(block_args):
        block_index, block_usable = block_args
        weights = slot_counts(block_index, block_usable, width).astype(jnp.bfloat16)
        return jnp.dot(weights, source_rows, preferred_element_type=jnp.float32)

    summed = lax.map(gather_one_block, (index_blocks, usable_blocks))
    return summed.reshape(node_rows, source_rows.shape[1])


def scatter_rows(table_size, index, usable, edge_weight):
    node_rows = index.shape[0]
    block_rows = min(512, node_rows)
    blocks = node_rows // block_rows
    index_blocks = index.reshape(blocks, block_rows, index.shape[1])
    usable_blocks = usable.reshape(blocks, block_rows, usable.shape[1])
    weight_blocks = edge_weight.reshape(blocks, block_rows, edge_weight.shape[1])

    def scatter_one_block(running, block_args):
        block_index, block_usable, block_weight = block_args
        weights = slot_counts(block_index, block_usable, table_size)
        added = lax.dot_general(
            weights,
            block_weight,
            (((0,), (0,)), ((), ())),
            precision=lax.Precision.HIGHEST,
            preferred_element_type=jnp.float32,
        )
        return (running + added, None)

    initial = jnp.zeros((table_size, edge_weight.shape[1]), jnp.float32)
    result, unused = lax.scan(
        scatter_one_block, initial, (index_blocks, usable_blocks, weight_blocks)
    )
    return result


def body(
    features, self_weight, neighbour_weight, send_lists, hub_nodes, neighbours, counts, cotangent
):
    node_dev = features.shape[0]
    feature_width = features.shape[1]
    peer_count = lax.axis_size("dom")
    per_peer = send_lists.shape[2]
    hub_count = hub_nodes.shape[1]
    lists_flat = send_lists[0].reshape(-1)
    hub_ids = hub_nodes[0]
    outgoing = jnp.take(features, lists_flat, axis=0).reshape(peer_count, per_peer, feature_width)
    hub_local = jnp.take(features, hub_ids, axis=0)
    repeated = jnp.broadcast_to(hub_local[None], (peer_count, hub_count, feature_width))
    packed = jnp.concatenate([outgoing, repeated], axis=1)
    arrived = lax.all_to_all(packed, "dom", split_axis=0, concat_axis=0, tiled=True)
    received = arrived[:, :per_peer]
    hub_table = arrived[:, per_peer:].reshape(peer_count * hub_count, feature_width)
    remote_rows = jnp.concatenate(
        [received.reshape(peer_count * per_peer, feature_width), hub_table], axis=0
    )
    usable = jnp.arange(neighbours.shape[1], dtype=jnp.int32)[None, :] < counts[:, None]
    whole_table = jnp.concatenate([features, remote_rows], axis=0)
    summed = gather_sum(whole_table, neighbours, usable)
    degree = counts.astype(jnp.float32)[:, None]
    mean = (summed / degree).astype(jnp.bfloat16)
    pre = jnp.dot(features, self_weight, preferred_element_type=jnp.float32) + jnp.dot(
        mean, neighbour_weight, preferred_element_type=jnp.float32
    )
    sigmoid_pre = jax.nn.sigmoid(pre)
    activations = (pre * sigmoid_pre).astype(jnp.bfloat16)
    grad_pre = (
        cotangent.astype(jnp.float32) * sigmoid_pre * (1.0 + pre * (1.0 - sigmoid_pre))
    ).astype(jnp.bfloat16)
    back_dims = (((1,), (1,)), ((), ()))
    grad_mean = lax.dot_general(
        grad_pre, neighbour_weight, back_dims, preferred_element_type=jnp.float32
    )
    grad_self = lax.dot_general(
        grad_pre, self_weight, back_dims, preferred_element_type=jnp.float32
    )
    edge_weight = grad_mean / degree
    remote_size = remote_rows.shape[0]
    table_grads = scatter_rows(node_dev + remote_size, neighbours, usable, edge_weight)
    local_grads = table_grads[:node_dev]
    remote_grads = table_grads[node_dev:]
    boundary_part = remote_grads[: peer_count * per_peer].reshape(
        peer_count, per_peer, feature_width
    )
    hub_part = remote_grads[peer_count * per_peer :]
    packed_grads = jnp.concatenate(
        [boundary_part, hub_part.reshape(peer_count, hub_count, feature_width)], axis=1
    )
    returned = lax.all_to_all(
        packed_grads.astype(jnp.bfloat16), "dom", split_axis=0, concat_axis=0, tiled=True
    ).astype(packed_grads.dtype)
    boundary_back = returned[:, :per_peer]
    hub_back = jnp.sum(returned[:, per_peer:], axis=0)
    grad_features = grad_self + local_grads
    grad_features = grad_features.at[lists_flat].add(
        boundary_back.reshape(peer_count * per_peer, feature_width)
    )
    grad_features = grad_features.at[hub_ids].add(hub_back)
    stacked = jnp.concatenate([features, mean], axis=1)
    grad_weights = lax.psum_scatter(
        lax.dot_general(
            stacked, grad_pre, (((0,), (0,)), ((), ())), preferred_element_type=jnp.float32
        ),
        "dom",
        scatter_dimension=0,
        tiled=True,
    )
    return (activations, grad_features, grad_weights)


def solution(mesh):
    in_specs = (
        P("dom", None),
        P(),
        P(),
        P("dom", None, None),
        P("dom", None),
        P("dom", None),
        P("dom"),
        P("dom", None),
    )
    out_specs = (P("dom", None), P("dom", None), P("dom", None))
    return jax.shard_map(body, mesh=mesh, in_specs=in_specs, out_specs=out_specs, check_vma=False)
```

profile of v0, /device:TPU:1, one launch (start us, length us, event | category | flops | bytes accessed | tf_op | source)
XLA Modules:
  0.0 697.9 jit_solution(6150906752643896052)
XLA Ops:
  7.2 0.7 fusion.19
  7.9 0.7 compare_and_fusion.1
  8.5 0.7 compare_and_fusion
  9.2 0.8 copy.33
  10.0 0.1 copy.32
  10.3 1.9 gather_fusion.1
  12.2 4.8 gather_fusion
  17.1 0.2 bitcast_select_fusion
  17.4 1.1 pad_maximum_fusion.1
  18.5 11.5 %all-to-all-start = ((bf16[128,16,256]{2,1,0:T(8,128)(2,1)}), bf16[128,16,256]{2,1,0:T(8,128)(2,1)S(1)}, u32[]{:S(2)}, u32[]{:S(2)}) async-start(bf16[128,16,256]{2,1,0:T(8,128)(2,1)} %pad_maximum_fusion.1), calls=%async_computation | async-start | bytes 2097152 | tf_op jit(solution)/shard_map/all_to_all | solution.py:71
  30.1 1.7 fusion.21
  31.8 17.4 %all-to-all-done = bf16[128,16,256]{2,1,0:T(8,128)(2,1)S(1)} async-done(((bf16[128,16,256]{2,1,0:T(8,128)(2,1)}), bf16[128,16,256]{2,1,0:T(8,128)(2,1)S(1)}, u32[]{:S(2)}, u32[]{:S(2)}) %all-to-all-start) | async-done | bytes 1048608 | tf_op jit(solution)/shard_map/all_to_all | solution.py:71
  49.3 1.5 pad_maximum_fusion
  50.8 195.5 %while.21 = (s32[]{:T(128)}, f32[4,512,256]{2,1,0:T(8,128)}, s32[4,512,16]{1,2,0:T(8,128)S(1)}, pred[4,512,16]{1,2,0:T(8,128)(4,1)S(1)}, bf16[4096,256]{1,0:T(8,128)(2,1)}, /*index=5*/s32[]{:T(128)}) while((s32[]{:T(128)}, f32[4,512,256]{2,1,0:T(8,128)}, s32[4,512,16]{1,2,0:T(8,128)S(1)}, pred[4,512,16]{1,2,0:T(8,128)(4,1)S(1)}, ...), condition=%wide.region_2.3_spmd, body=%wide.region_0.0_spmd.sunk | while | flops 1205862400 | bytes 11214937 | solution.py:26
  50.8 0.2 copy.44
  51.0 0.1 copy.43
  51.1 44.9 %convert_reduce_fusion.4 = bf16[512,4096]{1,0:T(8,128)(2,1)S(1)} fusion(s32[512,16]{1,0:T(8,128)S(1)} %copy.43, pred[512,16]{1,0:T(8,128)(4,1)S(1)} %copy.44), kind=kLoop, calls=%fused_computation.4.clone.1 | loop fusion | flops 132120576 | bytes 4235264 | tf_op jit(solution)/shard_map/while/body/eval_jaxpr/reduce_sum | solution.py:10
  96.0 3.7 fusion.41
  99.7 0.2 copy.44
  99.9 0.1 copy.43
  100.0 44.9 %convert_reduce_fusion.4 = bf16[512,4096]{1,0:T(8,128)(2,1)S(1)} fusion(s32[512,16]{1,0:T(8,128)S(1)} %copy.43, pred[512,16]{1,0:T(8,128)(4,1)S(1)} %copy.44), kind=kLoop, calls=%fused_computation.4.clone.1 | loop fusion | flops 132120576 | bytes 4235264 | tf_op jit(solution)/shard_map/while/body/eval_jaxpr/reduce_sum | solution.py:10
  144.9 3.7 fusion.41
  148.6 0.2 copy.44
  148.8 0.1 copy.43
  148.9 44.9 %convert_reduce_fusion.4 = bf16[512,4096]{1,0:T(8,128)(2,1)S(1)} fusion(s32[512,16]{1,0:T(8,128)S(1)} %copy.43, pred[512,16]{1,0:T(8,128)(4,1)S(1)} %copy.44), kind=kLoop, calls=%fused_computation.4.clone.1 | loop fusion | flops 132120576 | bytes 4235264 | tf_op jit(solution)/shard_map/while/body/eval_jaxpr/reduce_sum | solution.py:10
  193.8 3.7 fusion.41
  197.5 0.2 copy.44
  197.6 0.1 copy.43
  197.8 44.9 %convert_reduce_fusion.4 = bf16[512,4096]{1,0:T(8,128)(2,1)S(1)} fusion(s32[512,16]{1,0:T(8,128)S(1)} %copy.43, pred[512,16]{1,0:T(8,128)(4,1)S(1)} %copy.44), kind=kLoop, calls=%fused_computation.4.clone.1 | loop fusion | flops 132120576 | bytes 4235264 | tf_op jit(solution)/shard_map/while/body/eval_jaxpr/reduce_sum | solution.py:10
  242.7 3.6 fusion.41
  246.3 2.1 fusion.17
  248.6 0.3 copy-done.12
  248.8 2.2 multiply_convert_fusion
  251.1 1.8 convolution_divide_fusion
  252.9 263.3 %while.22 = (s32[]{:T(128)}, f32[4096,256]{1,0:T(8,128)}, s32[4,512,16]{1,2,0:T(8,128)S(1)}, pred[4,512,16]{1,2,0:T(8,128)(4,1)S(1)}, f32[4,512,256]{2,1,0:T(8,128)}, /*index=5*/s32[]{:T(128)}, s32[]{:T(128)}) while((s32[]{:T(128)}, f32[4096,256]{1,0:T(8,128)}, s32[4,512,16]{1,2,0:T(8,128)S(1)}, pred[4,512,16]{1,2,0:T(8,128)(4,1)S(1)}, ...), condition=%wide.region_5.6_spmd.clone, body=%wide.region_3.5_spmd.clone.sunk | while | flops 6576668672 | bytes 59449504 | solution.py:51
  252.9 0.2 copy.46
  253.0 0.1 copy.45
  253.2 47.7 %convert_reduce_fusion.5 = f32[512,4096]{1,0:T(8,128)} fusion(s32[512,16]{1,0:T(8,128)S(1)} %copy.45, pred[512,16]{1,0:T(8,128)(4,1)S(1)} %copy.46), kind=kLoop, calls=%fused_computation.13.clone.1 | loop fusion | flops 132120576 | bytes 8429568 | tf_op jit(solution)/shard_map/while/body/eval_jaxpr/reduce_sum | solution.py:10
  300.9 15.8 %convolution_add_fusion.4 = f32[4096,256]{1,0:T(8,128)S(1)} fusion(f32[512,4096]{1,0:T(8,128)} %convert_reduce_fusion.5, f32[4096,256]{1,0:T(8,128)S(1)} %copy-done.1, pred[]{:T(512)S(6)} %compare.3, f32[4,512,256]{2,1,0:T(8,128)} %get-tuple-element.231, s32[]{:T(128)S(6)} %copy.56), kind=kOutput, calls=%fused_computation.16.clone.1 | convolution fusion | flops 6444548096 | bytes 17301508 | tf_op jit(solution)/shard_map/while/body/eval_jaxpr/dot_general | solution.py:41
  316.7 2.0 copy-done.2
  318.7 0.2 copy.46
  318.9 0.1 copy.45
  319.0 47.7 %convert_reduce_fusion.5 = f32[512,4096]{1,0:T(8,128)} fusion(s32[512,16]{1,0:T(8,128)S(1)} %copy.45, pred[512,16]{1,0:T(8,128)(4,1)S(1)} %copy.46), kind=kLoop, calls=%fused_computation.13.clone.1 | loop fusion | flops 132120576 | bytes 8429568 | tf_op jit(solution)/shard_map/while/body/eval_jaxpr/reduce_sum | solution.py:10
  366.8 15.8 %convolution_add_fusion.4 = f32[4096,256]{1,0:T(8,128)S(1)} fusion(f32[512,4096]{1,0:T(8,128)} %convert_reduce_fusion.5, f32[4096,256]{1,0:T(8,128)S(1)} %copy-done.1, pred[]{:T(512)S(6)} %compare.3, f32[4,512,256]{2,1,0:T(8,128)} %get-tuple-element.231, s32[]{:T(128)S(6)} %copy.56), kind=kOutput, calls=%fused_computation.16.clone.1 | convolution fusion | flops 6444548096 | bytes 17301508 | tf_op jit(solution)/shard_map/while/body/eval_jaxpr/dot_general | solution.py:41
  382.6 2.0 copy-done.2
  384.5 0.2 copy.46
  384.8 47.7 %convert_reduce_fusion.5 = f32[512,4096]{1,0:T(8,128)} fusion(s32[512,16]{1,0:T(8,128)S(1)} %copy.45, pred[512,16]{1,0:T(8,128)(4,1)S(1)} %copy.46), kind=kLoop, calls=%fused_computation.13.clone.1 | loop fusion | flops 132120576 | bytes 8429568 | tf_op jit(solution)/shard_map/while/body/eval_jaxpr/reduce_sum | solution.py:10
  432.6 15.8 %convolution_add_fusion.4 = f32[4096,256]{1,0:T(8,128)S(1)} fusion(f32[512,4096]{1,0:T(8,128)} %convert_reduce_fusion.5, f32[4096,256]{1,0:T(8,128)S(1)} %copy-done.1, pred[]{:T(512)S(6)} %compare.3, f32[4,512,256]{2,1,0:T(8,128)} %get-tuple-element.231, s32[]{:T(128)S(6)} %copy.56), kind=kOutput, calls=%fused_computation.16.clone.1 | convolution fusion | flops 6444548096 | bytes 17301508 | tf_op jit(solution)/shard_map/while/body/eval_jaxpr/dot_general | solution.py:41
  448.4 2.0 copy-done.2
  450.4 0.2 copy.46
  450.7 47.7 %convert_reduce_fusion.5 = f32[512,4096]{1,0:T(8,128)} fusion(s32[512,16]{1,0:T(8,128)S(1)} %copy.45, pred[512,16]{1,0:T(8,128)(4,1)S(1)} %copy.46), kind=kLoop, calls=%fused_computation.13.clone.1 | loop fusion | flops 132120576 | bytes 8429568 | tf_op jit(solution)/shard_map/while/body/eval_jaxpr/reduce_sum | solution.py:10
  498.4 15.8 %convolution_add_fusion.4 = f32[4096,256]{1,0:T(8,128)S(1)} fusion(f32[512,4096]{1,0:T(8,128)} %convert_reduce_fusion.5, f32[4096,256]{1,0:T(8,128)S(1)} %copy-done.1, pred[]{:T(512)S(6)} %compare.3, f32[4,512,256]{2,1,0:T(8,128)} %get-tuple-element.231, s32[]{:T(128)S(6)} %copy.56), kind=kOutput, calls=%fused_computation.16.clone.1 | convolution fusion | flops 6444548096 | bytes 17301508 | tf_op jit(solution)/shard_map/while/body/eval_jaxpr/dot_general | solution.py:41
  514.2 2.0 copy-done.2
  516.2 2.4 convert.8
  518.7 1.0 pad_maximum_fusion.2
  519.7 4.6 all-to-all-start.1
  524.4 2.8 fusion.13
  527.2 3.7 convolution_add_fusion.1
  530.9 146.0 %all-reduce.3.cloned.1.call-done = f32[512,256]{1,0:T(8,128)} async-done(((f32[512,256]{1,0:T(8,128)}), f32[512,256]{1,0:T(8,128)}) %all-reduce.3.cloned.1.call-update) | async-done | bytes 524304
  676.9 1.3 constant_dynamic-slice_fusion
  678.2 0.3 convert_element_type.33
  678.5 0.1 slice_reduce_fusion
  678.6 9.0 %scatter_custom_fusion = f32[2048,256]{1,0:T(8,128)} fusion(f32[2048,256]{1,0:T(8,128)} %convolution_add_fusion.1, s32[1024]{0:T(1024)S(1)} %bitcast.82, f32[128,16,256]{2,1,0:T(8,128)S(1)} %convert_element_type.33), kind=kCustom, calls=%fused_computation.37 | custom fusion | flops 262144 | bytes 3145728 | tf_op jit(solution)/shard_map/scatter-add | solution.py:115
  687.6 3.5 scatter_fusion
  (68 shorter events, 1.0 us)
Async XLA Ops:
  7.2 241.3 %copy-start = (bf16[256,256]{1,0:T(8,128)(2,1)S(1)}, bf16[256,256]{1,0:T(8,128)(2,1)}, u32[]{:S(2)}) copy-start(bf16[256,256]{1,0:T(8,128)(2,1)} %param.14) | copy-start | bytes 393220
  17.4 12.6 %copy-start.11 = (s32[2048]{0:T(1024)S(1)}, s32[2048]{0:T(1024)}, u32[]{:S(2)}) copy-start(s32[2048]{0:T(1024)} %param.18) | copy-start | bytes 24580
  17.4 12.6 %copy-start.10 = (s32[2048,16]{0,1:T(8,128)S(1)}, s32[2048,16]{0,1:T(8,128)}, u32[]{:S(2)}) copy-start(s32[2048,16]{0,1:T(8,128)} %param.17) | copy-start | bytes 393220
  17.4 12.7 %copy-start.3 = (bf16[2048,256]{1,0:T(8,128)(2,1)S(1)}, bf16[2048,256]{1,0:T(8,128)(2,1)}, u32[]{:S(2)}) copy-start(bf16[2048,256]{1,0:T(8,128)(2,1)} %param.12) | copy-start | bytes 3145732
  17.4 12.7 %copy-start.9 = (bf16[256,256]{1,0:T(8,128)(2,1)S(1)}, bf16[256,256]{1,0:T(8,128)(2,1)}, u32[]{:S(2)}) copy-start(bf16[256,256]{1,0:T(8,128)(2,1)} %param.13) | copy-start | bytes 393220
  18.5 30.8 %all-to-all-start = ((bf16[128,16,256]{2,1,0:T(8,128)(2,1)}), bf16[128,16,256]{2,1,0:T(8,128)(2,1)S(1)}, u32[]{:S(2)}, u32[]{:S(2)}) async-start(bf16[128,16,256]{2,1,0:T(8,128)(2,1)} %pad_maximum_fusion.1), calls=%async_computation | async-start | bytes 2097152 | tf_op jit(solution)/shard_map/all_to_all | solution.py:71
  246.3 2.2 copy-start.5
  246.3 2.5 copy-start.12
  248.8 2.2 copy-start.6
  251.1 1.8 copy-start.8
  253.2 47.8 %copy-start.1 = (f32[4096,256]{1,0:T(8,128)S(1)}, f32[4096,256]{1,0:T(8,128)}, u32[]{:S(2)}) copy-start(f32[4096,256]{1,0:T(8,128)} %get-tuple-element.221) | copy-start | bytes 12582916 | tf_op jit(solution)/shard_map/while
  316.7 2.0 copy-start.2
  319.0 47.8 %copy-start.1 = (f32[4096,256]{1,0:T(8,128)S(1)}, f32[4096,256]{1,0:T(8,128)}, u32[]{:S(2)}) copy-start(f32[4096,256]{1,0:T(8,128)} %get-tuple-element.221) | copy-start | bytes 12582916 | tf_op jit(solution)/shard_map/while
  382.6 2.0 copy-start.2
  384.8 47.8 %copy-start.1 = (f32[4096,256]{1,0:T(8,128)S(1)}, f32[4096,256]{1,0:T(8,128)}, u32[]{:S(2)}) copy-start(f32[4096,256]{1,0:T(8,128)} %get-tuple-element.221) | copy-start | bytes 12582916 | tf_op jit(solution)/shard_map/while
  448.4 2.0 copy-start.2
  450.7 47.8 %copy-start.1 = (f32[4096,256]{1,0:T(8,128)S(1)}, f32[4096,256]{1,0:T(8,128)}, u32[]{:S(2)}) copy-start(f32[4096,256]{1,0:T(8,128)} %get-tuple-element.221) | copy-start | bytes 12582916 | tf_op jit(solution)/shard_map/while
  514.2 2.0 copy-start.2
  518.7 5.7 copy-start.4
  518.7 5.7 copy-start.7
  519.7 158.4 %all-to-all-start.1 = ((bf16[128,16,256]{2,1,0:T(8,128)(2,1)}), bf16[128,16,256]{2,1,0:T(8,128)(2,1)S(1)}, u32[]{:S(2)}, u32[]{:S(2)}) async-start(bf16[128,16,256]{2,1,0:T(8,128)(2,1)} %pad_maximum_fusion.2), calls=%async_computation.1 | async-start | bytes 2097152 | tf_op jit(solution)/shard_map/all_to_all | solution.py:109
  524.3 152.5 %all-reduce.3.cloned.1.call-start = ((), (), s32[]{:S(2)}) async-start(), calls=%async_computation.2 | async-start | bytes 1048576
Sparse Core Ops, SparseCore 0:
  529.9 146.9 all-reduce.2
where the time goes:
time: 699 us; the launch traced here: 698 us
  other arithmetic  394 us (56%)
  waiting for transfers between devices  163 us (23%)
  matrix products  90.1 us (13%)
  local copies, waits for them, and re-layouts  19.9 us (3%)
  starting transfers between devices  16.1 us (2%)
  between operations  14.3 us (2%)
    reduce_sum x8, other arithmetic, slot_counts(): return jnp.sum(hits.astype(jnp.float32), axis=1)  371 us
    unnamed x2, waiting for transfers between devices  146 us
    dot_general x4, matrix products, scatter_one_block(): lax.dot_general(weights, block_weight, (((0,), (0,)), ((), ())), precisio...  63.2 us
    all_to_all x1, waiting for transfers between devices, body(): lax.all_to_all(packed, 'dom', split_axis=0, concat_axis=0, tiled=True)  17.4 us
    dot_general x4, matrix products, gather_one_block(): return jnp.dot(weights, source_rows, preferred_element_type=jnp.float32)  14.6 us
  transfers between devices with their start and end apart: 3, of which 2 were waited for; matrix products, arithmetic and copies ran while one was open for 1% of the time, Pallas kernels for 0%

commit v1 on v0

v1 whole, which is shorter than its diff:
```python
import jax
import jax.numpy as jnp
from jax import lax
from jax.experimental import pallas as pl
from jax.experimental.pallas import tpu as pltpu
from jax.sharding import PartitionSpec as P

BF16 = jnp.bfloat16
F32 = jnp.float32
I32 = jnp.int32
NODES = 2048
WIDTH = 256
PEERS = 128
SLOTS = 16
FAN = 16
GROUPS = NODES // 16
LOCAL = 8
REMOTE = 8
VMEM = pl.BlockSpec(memory_space=pltpu.VMEM)
NN = (((1,), (0,)), ((), ()))
NT = (((1,), (1,)), ((), ()))
TN = (((0,), (0,)), ((), ()))


def dot(a, b, dims=NN):
    return lax.dot_general(a, b, dims, preferred_element_type=F32)


def one_hot(keys, shape, axis):
    return jnp.where(keys == lax.broadcasted_iota(I32, shape, axis), F32(1), F32(0)).astype(BF16)


def hub_column(hub):
    shape = (8, 8)
    diagonal = lax.broadcasted_iota(I32, shape, 0) == lax.broadcasted_iota(I32, shape, 1)
    spread = jnp.where(diagonal, jnp.broadcast_to(hub, shape), 0).astype(F32)
    return jnp.sum(spread, axis=1, keepdims=True).astype(I32)


def pack_kernel(features, lists, hub, packed, hot, rows):
    by_peer = lists[...].astype(F32).T.astype(I32)
    for slot in range(8):
        hot[slot * PEERS : (slot + 1) * PEERS, :] = one_hot(
            by_peer[:, slot : slot + 1], (PEERS, NODES), 1
        )
    hub_rows = one_hot(hub_column(hub[...]), (8, NODES), 1)
    hot[8 * PEERS : 8 * PEERS + 16, :] = jnp.concatenate(
        [hub_rows, jnp.zeros((8, NODES), BF16)], axis=0
    )
    picked = dot(hot[...], features[...])
    for slot in range(8):
        block = picked[slot * PEERS : (slot + 1) * PEERS]
        rows[0, pl.ds(slot, PEERS, stride=8), :] = block[:, :PEERS]
        rows[1, pl.ds(slot, PEERS, stride=8), :] = block[:, PEERS:]
    hubs = jnp.broadcast_to(picked[8 * PEERS : 8 * PEERS + 8][None], (PEERS, 8, WIDTH))
    bound = jnp.concatenate([rows[0], rows[1]], axis=1).reshape(PEERS, 8, WIDTH)
    packed[...] = jnp.concatenate([bound, hubs], axis=1).astype(BF16)


def pack(features, lists, hub):
    return pl.pallas_call(
        pack_kernel,
        out_shape=jax.ShapeDtypeStruct((PEERS, SLOTS, WIDTH), BF16),
        in_specs=[VMEM] * 3,
        out_specs=VMEM,
        scratch_shapes=[
            pltpu.VMEM((8 * PEERS + 16, NODES), BF16),
            pltpu.VMEM((2, 8 * PEERS, PEERS), F32),
        ],
        compiler_params=pltpu.CompilerParams(vmem_limit_bytes=24 << 20),
        cost_estimate=pl.CostEstimate(
            flops=2 * 1040 * NODES * WIDTH, bytes_accessed=2 << 20, transcendentals=0
        ),
        name="pack",
    )(features, lists, hub)


def flatten_lanes(values):
    n = values.shape[1]
    spread = jnp.where(
        lax.broadcasted_iota(I32, (16, 256), 0) == (lax.broadcasted_iota(I32, (16, 256), 1) & 15),
        F32(1),
        F32(0),
    ).astype(BF16)
    tiled = dot(values.astype(BF16), spread, TN).reshape(n // 16, 16, 256)
    shape = (n // 16, 16, 256)
    mine = (lax.broadcasted_iota(I32, shape, 2) >> 4) == lax.broadcasted_iota(I32, shape, 1)
    return jnp.sum(jnp.where(mine, tiled, F32(0)), axis=1)


def count_kernel(neighbours, counts, features, self_weight, table, summed, pre, key_hi, key_lo):
    index = neighbours[...]
    bound = index - NODES
    hub = bound - 8 * PEERS
    index = jnp.where(
        index < NODES,
        index,
        jnp.where(
            hub < 0,
            NODES + ((bound >> 3) << 4) + (bound & 7),
            NODES + ((hub >> 3) << 4) + 8 + (hub & 7),
        ),
    )
    usable = lax.broadcasted_iota(I32, index.shape, 0) < counts[...]
    index = jnp.where(usable, index, 4096)
    lane = lax.broadcasted_iota(I32, (GROUPS, 256), 1)
    key_hi[...] = flatten_lanes((index >> 8).astype(F32)) * 16.0 + (lane >> 4).astype(F32)
    key_lo[...] = flatten_lanes((index & 255).astype(F32))

    def one_group(group, carry):
        rows = lax.broadcasted_iota(I32, (256, 256), 0).astype(F32).astype(BF16)
        hi = jnp.broadcast_to(key_hi[pl.ds(group, 1), :].astype(BF16), (256, 256))
        lo = jnp.broadcast_to(key_lo[pl.ds(group, 1), :].astype(BF16), (256, 256))
        left = jnp.where(hi == rows, BF16(1), BF16(0))
        right = jnp.where(lo == rows, BF16(1), BF16(0))
        block = dot(left, right, NT).astype(BF16)
        table[:, pl.ds(pl.multiple_of(group * 16, 16), 16), :] = block.reshape(16, 16, 256)
        return carry

    lax.fori_loop(0, GROUPS, one_group, 0, unroll=16)

    def one_block(step, carry):
        at = pl.ds(pl.multiple_of(step * 512, 512), 512)
        total = jnp.zeros((512, WIDTH), F32)
        for hi in range(LOCAL):
            total = total + dot(table[hi, at, :], features[hi * 256 : (hi + 1) * 256, :])
        summed[at, :] = total
        pre[at, :] = dot(features[at, :], self_weight[...])
        return carry

    lax.fori_loop(0, NODES // 512, one_block, 0)


def count(neighbours, counts, features, self_weight):
    return pl.pallas_call(
        count_kernel,
        out_shape=(
            pltpu.VMEM((LOCAL + REMOTE, NODES, WIDTH), BF16),
            pltpu.VMEM((NODES, WIDTH), F32),
            pltpu.VMEM((NODES, WIDTH), F32),
        ),
        in_specs=[VMEM] * 4,
        out_specs=[VMEM] * 3,
        scratch_shapes=[pltpu.VMEM((GROUPS, 256), F32)] * 2,
        compiler_params=pltpu.CompilerParams(vmem_limit_bytes=12 << 20),
        cost_estimate=pl.CostEstimate(
            flops=2 * NODES * 4096 * WIDTH * 2, bytes_accessed=2 << 20, transcendentals=0
        ),
        name="count",
    )(neighbours, counts, features, self_weight)


def node_kernel(
    arrived,
    table,
    summed,
    pre_self,
    features,
    counts,
    cotangent,
    neighbour_weight,
    activations,
    grad_pre,
    edge,
    message,
    mean,
    weights,
    parts,
):
    inverse = (1.0 / counts[...].astype(F32)).T
    remote = arrived[...].reshape(NODES, WIDTH)
    for block in range(NODES // 256):
        at = slice(block * 256, (block + 1) * 256)
        total = summed[at, :]
        for hi in range(REMOTE):
            total = total + dot(table[LOCAL + hi, at, :], remote[hi * 256 : (hi + 1) * 256])
        scale = jnp.concatenate(
            [
                jnp.broadcast_to(inverse[:, 2 * block + half : 2 * block + half + 1], (128, 256))
                for half in range(2)
            ],
            axis=0,
        )
        block_mean = (total * scale).astype(BF16)
        mean[at, :] = block_mean
        pre = pre_self[at, :] + dot(block_mean, neighbour_weight[...])
        sigmoid = 1.0 / (1.0 + jnp.exp(-pre))
        activations[at, :] = (pre * sigmoid).astype(BF16)
        slope = sigmoid * (1.0 + pre * (1.0 - sigmoid))
        block_grad = (cotangent[at, :].astype(F32) * slope).astype(BF16)
        grad_pre[at, :] = block_grad
        edge[at, :] = (dot(block_grad, neighbour_weight[...], NT) * scale).astype(BF16)
    for hi in range(REMOTE):
        added = dot(table[LOCAL + hi], edge[...], TN).astype(BF16).reshape(16, 16, WIDTH)
        message[hi * 16 : (hi + 1) * 16, 0:16, :] = added[:, :, :128]
        message[hi * 16 : (hi + 1) * 16, 16:32, :] = added[:, :, 128:]
    for part, rows in ((0, features), (1, mean)):
        block = dot(rows[...], grad_pre[...], TN)
        weights[0, part * WIDTH : (part + 1) * WIDTH, :] = block[:, :128]
        weights[1, part * WIDTH : (part + 1) * WIDTH, :] = block[:, 128:]
    for half in range(2):
        for row in range(4):
            value = weights[half, pl.ds(row, PEERS, stride=4), :]
            high = value.astype(BF16).astype(F32)
            parts[pl.ds(half * 4 + row, PEERS, stride=16), :] = high
            parts[pl.ds(8 + half * 4 + row, PEERS, stride=16), :] = value - high
    message[:, 32:48, :] = parts[...].astype(BF16).reshape(PEERS, 16, 128)


def node(arrived, table, summed, pre_self, features, counts, cotangent, neighbour_weight):
    return pl.pallas_call(
        node_kernel,
        out_shape=(
            jax.ShapeDtypeStruct((NODES, WIDTH), BF16),
            pltpu.VMEM((NODES, WIDTH), BF16),
            pltpu.VMEM((NODES, WIDTH), BF16),
            jax.ShapeDtypeStruct((PEERS, 48, 128), BF16),
        ),
        in_specs=[VMEM] * 8,
        out_specs=[VMEM] * 4,
        scratch_shapes=[
            pltpu.VMEM((NODES, WIDTH), BF16),
            pltpu.VMEM((2, 2 * WIDTH, 128), F32),
            pltpu.VMEM((NODES, 128), F32),
        ],
        compiler_params=pltpu.CompilerParams(vmem_limit_bytes=20 << 20),
        cost_estimate=pl.CostEstimate(
            flops=2 * NODES * 2048 * WIDTH * 2, bytes_accessed=6 << 20, transcendentals=0
        ),
        name="node",
    )(arrived, table, summed, pre_self, features, counts, cotangent, neighbour_weight)


def local_kernel(table, edge, grad_pre, self_weight, lists, hub, grads, hot, ids):
    for hi in range(LOCAL):
        at = slice(hi * 256, (hi + 1) * 256)
        grads[at, :] = dot(table[hi], edge[...], TN) + dot(grad_pre[at, :], self_weight[...], NT)
    slots = jnp.concatenate(
        [lists[...], jnp.broadcast_to(hub_column(hub[...]), (8, PEERS))], axis=0
    )
    ids[...] = flatten_lanes((slots >> 8).astype(F32)) * 256.0 + flatten_lanes(
        (slots & 255).astype(F32)
    )
    for chunk in range(8):
        row = jnp.broadcast_to(ids[chunk : chunk + 1, :].astype(I32), (NODES, 256))
        hot[:, chunk * 256 : (chunk + 1) * 256] = one_hot(row, (NODES, 256), 0)


def local(table, edge, grad_pre, self_weight, lists, hub):
    return pl.pallas_call(
        local_kernel,
        out_shape=(
            pltpu.VMEM((NODES, WIDTH), F32),
            pltpu.VMEM((NODES, PEERS * SLOTS), BF16),
        ),
        in_specs=[VMEM] * 6,
        out_specs=[VMEM] * 2,
        scratch_shapes=[pltpu.VMEM((8, 256), F32)],
        compiler_params=pltpu.CompilerParams(vmem_limit_bytes=12 << 20),
        cost_estimate=pl.CostEstimate(
            flops=2 * NODES * 2048 * WIDTH, bytes_accessed=2 << 20, transcendentals=0
        ),
        name="local",
    )(table, edge, grad_pre, self_weight, lists, hub)


def finish_kernel(returned, grads, hot, grad_features, grad_weights):
    back = jnp.concatenate([returned[:, 0:16, :], returned[:, 16:32, :]], axis=2)
    back = back.reshape(PEERS * SLOTS, WIDTH)
    grad_features[...] = grads[...] + dot(hot[...], back)
    parts = jnp.sum(returned[:, 32:48, :].astype(F32), axis=0)
    total = parts[:8] + parts[8:]
    grad_weights[...] = jnp.concatenate([total[:4], total[4:]], axis=1)


def finish(returned, grads, hot):
    return pl.pallas_call(
        finish_kernel,
        out_shape=(
            jax.ShapeDtypeStruct((NODES, WIDTH), F32),
            jax.ShapeDtypeStruct((4, WIDTH), F32),
        ),
        in_specs=[VMEM] * 3,
        out_specs=[VMEM] * 2,
        compiler_params=pltpu.CompilerParams(vmem_limit_bytes=16 << 20),
        cost_estimate=pl.CostEstimate(
            flops=2 * NODES * 2048 * WIDTH, bytes_accessed=4 << 20, transcendentals=0
        ),
        name="finish",
    )(returned, grads, hot)


def body(
    features, self_weight, neighbour_weight, send_lists, hub_nodes, neighbours, counts, cotangent
):
    lists = send_lists[0].T
    packed = pack(features, lists, hub_nodes)
    arrived = lax.all_to_all(packed, "dom", split_axis=0, concat_axis=0, tiled=True)
    table, summed, pre_self = count(
        neighbours.T, counts.reshape(1, NODES), features, self_weight
    )
    activations, grad_pre, edge, message = node(
        arrived,
        table,
        summed,
        pre_self,
        features,
        counts.reshape(16, 128),
        cotangent,
        neighbour_weight,
    )
    returned = lax.all_to_all(message, "dom", split_axis=0, concat_axis=0, tiled=True)
    grads, hot = local(table, edge, grad_pre, self_weight, lists, hub_nodes)
    grad_features, grad_weights = finish(returned, grads, hot)
    return (activations, grad_features, grad_weights)


def solution(mesh):
    in_specs = (
        P("dom", None),
        P(),
        P(),
        P("dom", None, None),
        P("dom", None),
        P("dom", None),
        P("dom"),
        P("dom", None),
    )
    out_specs = (P("dom", None), P("dom", None), P("dom", None))
    return jax.shard_map(body, mesh=mesh, in_specs=in_specs, out_specs=out_specs, check_vma=False)
```

time: 699 us -> 103 us (0.15)
  other arithmetic: 394 us -> 0 us
  waiting for transfers between devices: 163 us -> 7.21 us
  matrix products: 90.1 us -> 0 us
  Pallas kernels: 0 us -> 33.8 us
  local copies, waits for them, and re-layouts: 19.9 us -> 40.4 us
  between operations: 14.3 us -> 0.77 us
    reduce_sum x9 -> x0, other arithmetic: 371 us -> none  [the longest x8 371 us: slot_counts(): return jnp.sum(hits.astype(jnp.float32), axis=1)]
    unnamed x2 -> x0, waiting for transfers between devices: 146 us -> none
    dot_general x13 -> x0, matrix products: 90.1 us -> none  [the longest x4 63.2 us: scatter_one_block(): lax.dot_general(weights, block_weight, (((0,), (0,)), ((), ())), precisio...]
    unnamed x24 -> x52, local copies, waits for them, and re-layouts: 2.52 us -> 40.4 us
    pallas_call x0 -> x5, Pallas kernels: none -> 33.8 us  [the longest x1 10.6 us: node(): pl.pallas_call(node_kernel, out_shape=(jax.ShapeDtypeStruct((NODES, WIDTH...]
    all_to_all x1, waiting for transfers between devices: 17.4 us -> 0.71 us  [body(): lax.all_to_all(packed, 'dom', split_axis=0, concat_axis=0, tiled=True)]
    scatter-add x2 -> x0, other arithmetic: 12.5 us -> none  [the longest x1 8.97 us: body(): grad_features.at[lists_flat]]
    while x16 -> x0, local copies, waits for them, and re-layouts: 7.84 us -> none
  transfers between devices with their start and end apart: 3 -> 2, of which waited for: 2 -> 2; matrix products, arithmetic and copies ran while one was open for 1% -> 0% of each run, Pallas kernels for 0% -> 17%
where the time goes in v1:
time: 103 us
  local copies, waits for them, and re-layouts  40.4 us (39%)
  Pallas kernels  33.8 us (33%)
  starting transfers between devices  20.6 us (20%)
  waiting for transfers between devices  7.21 us (7%)
    unnamed x52, local copies, waits for them, and re-layouts  40.4 us
    all_to_all x1, starting transfers between devices, body(): lax.all_to_all(packed, 'dom', split_axis=0, concat_axis=0, tiled=True)  11.5 us
    pallas_call x1, Pallas kernels, node(): pl.pallas_call(node_kernel, out_shape=(jax.ShapeDtypeStruct((NODES, WIDTH...  10.6 us
    pallas_call x1, Pallas kernels, count(): pl.pallas_call(count_kernel, out_shape=(pltpu.VMEM((LOCAL + REMOTE, NODES...  10.2 us
    all_to_all x1, starting transfers between devices, body(): lax.all_to_all(message, 'dom', split_axis=0, concat_axis=0, tiled=True)  9.06 us
    pallas_call x1, Pallas kernels, local(): pl.pallas_call(local_kernel, out_shape=(pltpu.VMEM((NODES, WIDTH), F32),...  6.75 us
    all_to_all x1, waiting for transfers between devices, body(): lax.all_to_all(message, 'dom', split_axis=0, concat_axis=0, tiled=True)  6.5 us
    pallas_call x1, Pallas kernels, finish(): pl.pallas_call(finish_kernel, out_shape=(jax.ShapeDtypeStruct((NODES, WID...  3.68 us
  transfers between devices with their start and end apart: 2, of which 2 were waited for; matrix products, arithmetic and copies ran while one was open for 0% of the time, Pallas kernels for 17%

profile of v1, /device:TPU:1, one launch (start us, length us, event | category | flops | bytes accessed | tf_op | source)
XLA Modules:
  0.0 102.7 jit_solution(16192308883008868849)
XLA Ops:
  0.6 0.0 copy-start.10
  0.6 1.2 %copy-done.10 = bf16[2048,256]{1,0:T(8,128)(2,1)S(1)} copy-done((bf16[2048,256]{1,0:T(8,128)(2,1)S(1)}, bf16[2048,256]{1,0:T(8,128)(2,1)}, u32[]{:S(2)}) %copy-start.10) | copy-done | bytes 1048600
  1.9 0.0 copy-start.21
  1.9 0.7 copy-done.21
  2.5 0.0 copy-start.23
  2.5 0.7 copy-done.23
  3.2 0.0 copy-start.19
  3.2 0.0 copy-start.20
  3.2 0.0 copy-start.25
  3.2 2.5 %pack.1 = bf16[128,16,256]{2,1,0:T(8,128)(2,1)} custom-call(bf16[2048,256]{1,0:T(8,128)(2,1)S(1)} %copy-done.10, s32[8,128]{1,0:T(8,128)S(1)} %bitcast.8, s32[1,8]{1,0:T(1,128)S(1)} %copy-done.23), custom_call_target="tpu_custom_call" | custom-call | flops 1090519040 | bytes 2097152 | tf_op jit(solution)/shard_map/pack/pallas_call | solution.py:61
  5.7 11.5 %all-to-all-start = ((bf16[128,16,256]{2,1,0:T(8,128)(2,1)}), bf16[128,16,256]{2,1,0:T(8,128)(2,1)S(1)}, u32[]{:S(2)}, u32[]{:S(2)}) async-start(bf16[128,16,256]{2,1,0:T(8,128)(2,1)} %pack.1), calls=%async_computation | async-start | bytes 2097152 | tf_op jit(solution)/shard_map/all_to_all | solution.py:298
  17.2 0.0 copy-done.19
  17.2 0.0 copy-done.20
  17.2 0.0 copy-done.25
  17.3 0.0 copy-start.11
  17.3 1.2 %copy-done.11 = bf16[2048,256]{1,0:T(8,128)(2,1)S(1)} copy-done((bf16[2048,256]{1,0:T(8,128)(2,1)S(1)}, bf16[2048,256]{1,0:T(8,128)(2,1)}, u32[]{:S(2)}) %copy-start.11) | copy-done | bytes 1048600
  18.5 0.0 copy-start.18
  18.5 10.2 %count.1 = (bf16[16,2048,256]{2,1,0:T(8,128)(2,1)S(1)}, f32[2048,256]{1,0:T(8,128)S(1)}, f32[2048,256]{1,0:T(8,128)S(1)}) custom-call(s32[16,2048]{1,0:T(8,128)S(1)} %bitcast.10, s32[1,2048]{1,0:T(1,128)S(1)} %bitcast.6, bf16[2048,256]{1,0:T(8,128)(2,1)S(1)} %copy-done.11, bf16[256,256]{1,0:T(8,128)(2,1)S(1)} %copy-done.19), custom_call_target="tpu_custom_call" | custom-call | flops 8589934592 | bytes 2097152 | tf_op jit(solution)/shard_map/count/pallas_call | solution.py:135
  28.7 0.0 copy-start
  28.7 5.7 %copy-done = bf16[16,2048,256]{2,1,0:T(8,128)(2,1)} copy-done((bf16[16,2048,256]{2,1,0:T(8,128)(2,1)}, bf16[16,2048,256]{2,1,0:T(8,128)(2,1)S(1)}, u32[]{:S(2)}) %copy-start) | copy-done | bytes 16777240
  34.5 0.0 copy-start.7
  34.5 1.3 %copy-done.7 = f32[2048,256]{1,0:T(8,128)} copy-done((f32[2048,256]{1,0:T(8,128)}, f32[2048,256]{1,0:T(8,128)S(1)}, u32[]{:S(2)}) %copy-start.7) | copy-done | bytes 2097176
  35.8 0.7 all-to-all-done.arrived
  36.5 0.0 copy-done.18
  36.5 0.0 copy-start.1
  36.5 5.8 %copy-done.1 = bf16[16,2048,256]{2,1,0:T(8,128)(2,1)S(1)} copy-done((bf16[16,2048,256]{2,1,0:T(8,128)(2,1)S(1)}, bf16[16,2048,256]{2,1,0:T(8,128)(2,1)}, u32[]{:S(2)}) %copy-start.1) | copy-done | bytes 16777240
  42.3 0.0 copy-start.8
  42.3 1.6 %copy-done.8 = f32[2048,256]{1,0:T(8,128)S(1)} copy-done((f32[2048,256]{1,0:T(8,128)S(1)}, f32[2048,256]{1,0:T(8,128)}, u32[]{:S(2)}) %copy-start.8) | copy-done | bytes 2097176
  43.9 0.0 copy-start.12
  43.9 1.2 %copy-done.12 = bf16[2048,256]{1,0:T(8,128)(2,1)S(1)} copy-done((bf16[2048,256]{1,0:T(8,128)(2,1)S(1)}, bf16[2048,256]{1,0:T(8,128)(2,1)}, u32[]{:S(2)}) %copy-start.12) | copy-done | bytes 1048600
  45.1 0.0 copy-start.13
  45.1 1.2 %copy-done.13 = bf16[2048,256]{1,0:T(8,128)(2,1)S(1)} copy-done((bf16[2048,256]{1,0:T(8,128)(2,1)S(1)}, bf16[2048,256]{1,0:T(8,128)(2,1)}, u32[]{:S(2)}) %copy-start.13) | copy-done | bytes 1048600
  46.3 10.6 %node.1 = (bf16[2048,256]{1,0:T(8,128)(2,1)}, bf16[2048,256]{1,0:T(8,128)(2,1)S(1)}, bf16[2048,256]{1,0:T(8,128)(2,1)S(1)}, bf16[128,48,128]{2,1,0:T(8,128)(2,1)S(1)}) custom-call(bf16[128,16,256]{2,1,0:T(8,128)(2,1)S(1)} %all-to-all-done.arrived, bf16[16,2048,256]{2,1,0:T(8,128)(2,1)S(1)} %copy-done.1, f32[2048,256]{1,0:T(8,128)S(1)} %get-tuple-element.15.summed, ...), custom_call_target="tpu_custom_call" | custom-call | flops 4294967296 | bytes 6291456 | tf_op jit(solution)/shard_map/node/pallas_call | solution.py:211
  56.9 0.0 copy-start.9
  56.9 1.2 %copy-done.9 = bf16[128,48,128]{2,1,0:T(8,128)(2,1)} copy-done((bf16[128,48,128]{2,1,0:T(8,128)(2,1)}, bf16[128,48,128]{2,1,0:T(8,128)(2,1)S(1)}, u32[]{:S(2)}) %copy-start.9) | copy-done | bytes 1572888
  58.1 0.0 copy-start.14
  58.1 1.0 copy-done.14
  59.1 0.0 copy-start.16
  59.1 1.0 copy-done.16
  60.1 0.0 copy-start.22
  60.1 0.0 copy-start.24
  60.1 0.0 copy-start.15
  60.1 9.1 %all-to-all-start.1 = ((bf16[128,48,128]{2,1,0:T(8,128)(2,1)}), bf16[128,48,128]{2,1,0:T(8,128)(2,1)S(1)}, u32[]{:S(2)}, u32[]{:S(2)}) async-start(bf16[128,48,128]{2,1,0:T(8,128)(2,1)} %copy-done.9), calls=%async_computation.1 | async-start | bytes 3145728 | tf_op jit(solution)/shard_map/all_to_all | solution.py:312
  69.1 0.0 copy-done.22
  69.2 0.0 copy-done.24
  69.2 0.0 copy-done.15
  69.2 0.0 copy-start.2
  69.2 5.8 %copy-done.2 = bf16[16,2048,256]{2,1,0:T(8,128)(2,1)S(1)} copy-done((bf16[16,2048,256]{2,1,0:T(8,128)(2,1)S(1)}, bf16[16,2048,256]{2,1,0:T(8,128)(2,1)}, u32[]{:S(2)}) %copy-start.2) | copy-done | bytes 16777240
  74.9 0.0 copy-start.17
  75.0 1.2 %copy-done.17 = bf16[2048,256]{1,0:T(8,128)(2,1)S(1)} copy-done((bf16[2048,256]{1,0:T(8,128)(2,1)S(1)}, bf16[2048,256]{1,0:T(8,128)(2,1)}, u32[]{:S(2)}) %copy-start.17) | copy-done | bytes 1048600
  76.2 6.7 %local.1 = (f32[2048,256]{1,0:T(8,128)S(1)}, bf16[2048,2048]{1,0:T(8,128)(2,1)S(1)}) custom-call(bf16[16,2048,256]{2,1,0:T(8,128)(2,1)S(1)} %copy-done.2, bf16[2048,256]{1,0:T(8,128)(2,1)S(1)} %copy-done.17, bf16[2048,256]{1,0:T(8,128)(2,1)S(1)} %copy-done.15, bf16[256,256]{1,0:T(8,128)(2,1)S(1)} %copy-done.19, s32[8,128]{1,0:T(8,128)S(1)} %bitcast.9, ...), custom_call_target="tpu_custom_call" | custom-call | flops 2147483648 | bytes 2097152 | tf_op jit(solution)/shard_map/local/pallas_call | solution.py:250
  82.9 0.0 copy-start.3
  82.9 3.3 %copy-done.3 = bf16[2048,2048]{1,0:T(8,128)(2,1)} copy-done((bf16[2048,2048]{1,0:T(8,128)(2,1)}, bf16[2048,2048]{1,0:T(8,128)(2,1)S(1)}, u32[]{:S(2)}) %copy-start.3) | copy-done | bytes 8388632
  86.2 0.0 copy-start.5
  86.2 1.3 %copy-done.5 = f32[2048,256]{1,0:T(8,128)} copy-done((f32[2048,256]{1,0:T(8,128)}, f32[2048,256]{1,0:T(8,128)S(1)}, u32[]{:S(2)}) %copy-start.5) | copy-done | bytes 2097176
  87.5 6.5 %all-to-all-done.1.returned = bf16[128,48,128]{2,1,0:T(8,128)(2,1)S(1)} async-done(((bf16[128,48,128]{2,1,0:T(8,128)(2,1)}), bf16[128,48,128]{2,1,0:T(8,128)(2,1)S(1)}, u32[]{:S(2)}, u32[]{:S(2)}) %all-to-all-start.1) | async-done | bytes 1572896 | tf_op jit(solution)/shard_map/all_to_all | solution.py:312
  94.0 0.0 copy-start.4
  94.0 3.4 %copy-done.4 = bf16[2048,2048]{1,0:T(8,128)(2,1)S(1)} copy-done((bf16[2048,2048]{1,0:T(8,128)(2,1)S(1)}, bf16[2048,2048]{1,0:T(8,128)(2,1)}, u32[]{:S(2)}) %copy-start.4) | copy-done | bytes 8388632
  97.4 0.0 copy-start.6
  97.4 1.6 %copy-done.6 = f32[2048,256]{1,0:T(8,128)S(1)} copy-done((f32[2048,256]{1,0:T(8,128)S(1)}, f32[2048,256]{1,0:T(8,128)}, u32[]{:S(2)}) %copy-start.6) | copy-done | bytes 2097176
  99.0 3.7 %finish.1 = (f32[2048,256]{1,0:T(8,128)}, f32[4,256]{1,0:T(4,128)}) custom-call(bf16[128,48,128]{2,1,0:T(8,128)(2,1)S(1)} %all-to-all-done.1.returned, f32[2048,256]{1,0:T(8,128)S(1)} %copy-done.6, bf16[2048,2048]{1,0:T(8,128)(2,1)S(1)} %copy-done.4), custom_call_target="tpu_custom_call" | custom-call | flops 2147483648 | bytes 4194304 | tf_op jit(solution)/shard_map/finish/pallas_call | solution.py:277
Async XLA Ops:
  0.6 1.2 %copy-start.10 = (bf16[2048,256]{1,0:T(8,128)(2,1)S(1)}, bf16[2048,256]{1,0:T(8,128)(2,1)}, u32[]{:S(2)}) copy-start(bf16[2048,256]{1,0:T(8,128)(2,1)} %features.5) | copy-start | bytes 3145732
  1.9 0.7 copy-start.21
  2.5 0.7 copy-start.23
  3.2 14.0 %copy-start.19 = (bf16[256,256]{1,0:T(8,128)(2,1)S(1)}, bf16[256,256]{1,0:T(8,128)(2,1)}, u32[]{:S(2)}) copy-start(bf16[256,256]{1,0:T(8,128)(2,1)} %self_weight.3) | copy-start | bytes 393220
  3.2 14.0 %copy-start.20 = (s32[2048]{0:T(1024)S(1)}, s32[2048]{0:T(1024)}, u32[]{:S(2)}) copy-start(s32[2048]{0:T(1024)} %param.14) | copy-start | bytes 24580
  3.2 14.0 %copy-start.25 = (s32[2048,16]{0,1:T(8,128)S(1)}, s32[2048,16]{0,1:T(8,128)}, u32[]{:S(2)}) copy-start(s32[2048,16]{0,1:T(8,128)} %param.13) | copy-start | bytes 393220
  5.7 30.8 %all-to-all-start = ((bf16[128,16,256]{2,1,0:T(8,128)(2,1)}), bf16[128,16,256]{2,1,0:T(8,128)(2,1)S(1)}, u32[]{:S(2)}, u32[]{:S(2)}) async-start(bf16[128,16,256]{2,1,0:T(8,128)(2,1)} %pack.1), calls=%async_computation | async-start | bytes 2097152 | tf_op jit(solution)/shard_map/all_to_all | solution.py:298
  17.3 1.2 %copy-start.11 = (bf16[2048,256]{1,0:T(8,128)(2,1)S(1)}, bf16[2048,256]{1,0:T(8,128)(2,1)}, u32[]{:S(2)}) copy-start(bf16[2048,256]{1,0:T(8,128)(2,1)} %features.5) | copy-start | bytes 3145732
  18.5 18.0 %copy-start.18 = (bf16[256,256]{1,0:T(8,128)(2,1)S(1)}, bf16[256,256]{1,0:T(8,128)(2,1)}, u32[]{:S(2)}) copy-start(bf16[256,256]{1,0:T(8,128)(2,1)} %neighbour_weight.1) | copy-start | bytes 393220
  28.7 5.7 %copy-start = (bf16[16,2048,256]{2,1,0:T(8,128)(2,1)}, bf16[16,2048,256]{2,1,0:T(8,128)(2,1)S(1)}, u32[]{:S(2)}) copy-start(bf16[16,2048,256]{2,1,0:T(8,128)(2,1)S(1)} %get-tuple-element.14.table) | copy-start | bytes 50331652
  34.5 1.3 %copy-start.7 = (f32[2048,256]{1,0:T(8,128)}, f32[2048,256]{1,0:T(8,128)S(1)}, u32[]{:S(2)}) copy-start(f32[2048,256]{1,0:T(8,128)S(1)} %get-tuple-element.16.pre_self) | copy-start | bytes 6291460
  36.5 5.8 %copy-start.1 = (bf16[16,2048,256]{2,1,0:T(8,128)(2,1)S(1)}, bf16[16,2048,256]{2,1,0:T(8,128)(2,1)}, u32[]{:S(2)}) copy-start(bf16[16,2048,256]{2,1,0:T(8,128)(2,1)} %copy-done) | copy-start | bytes 50331652
  42.3 1.6 %copy-start.8 = (f32[2048,256]{1,0:T(8,128)S(1)}, f32[2048,256]{1,0:T(8,128)}, u32[]{:S(2)}) copy-start(f32[2048,256]{1,0:T(8,128)} %copy-done.7) | copy-start | bytes 6291460
  43.9 1.2 %copy-start.12 = (bf16[2048,256]{1,0:T(8,128)(2,1)S(1)}, bf16[2048,256]{1,0:T(8,128)(2,1)}, u32[]{:S(2)}) copy-start(bf16[2048,256]{1,0:T(8,128)(2,1)} %features.5) | copy-start | bytes 3145732
  45.1 1.2 %copy-start.13 = (bf16[2048,256]{1,0:T(8,128)(2,1)S(1)}, bf16[2048,256]{1,0:T(8,128)(2,1)}, u32[]{:S(2)}) copy-start(bf16[2048,256]{1,0:T(8,128)(2,1)} %cotangent.1) | copy-start | bytes 3145732
  56.9 1.2 %copy-start.9 = (bf16[128,48,128]{2,1,0:T(8,128)(2,1)}, bf16[128,48,128]{2,1,0:T(8,128)(2,1)S(1)}, u32[]{:S(2)}) copy-start(bf16[128,48,128]{2,1,0:T(8,128)(2,1)S(1)} %get-tuple-element.18) | copy-start | bytes 4718596
  58.1 1.0 copy-start.14
  59.1 1.0 copy-start.16
  60.1 9.1 %copy-start.22 = (s32[1,128,8]{1,2,0:T(8,128)S(1)}, s32[1,128,8]{1,2,0:T(8,128)}, u32[]{:S(2)}) copy-start(s32[1,128,8]{1,2,0:T(8,128)} %param.11) | copy-start | bytes 12292
  60.1 9.1 %copy-start.24 = (s32[1,8]{1,0:T(1,128)S(1)}, s32[1,8]{1,0:T(1,128)}, u32[]{:S(2)}) copy-start(s32[1,8]{1,0:T(1,128)} %hub.3) | copy-start | bytes 100
  60.1 9.1 %copy-start.15 = (bf16[2048,256]{1,0:T(8,128)(2,1)S(1)}, bf16[2048,256]{1,0:T(8,128)(2,1)}, u32[]{:S(2)}) copy-start(bf16[2048,256]{1,0:T(8,128)(2,1)} %copy-done.14) | copy-start | bytes 3145732
  60.1 34.0 %all-to-all-start.1 = ((bf16[128,48,128]{2,1,0:T(8,128)(2,1)}), bf16[128,48,128]{2,1,0:T(8,128)(2,1)S(1)}, u32[]{:S(2)}, u32[]{:S(2)}) async-start(bf16[128,48,128]{2,1,0:T(8,128)(2,1)} %copy-done.9), calls=%async_computation.1 | async-start | bytes 3145728 | tf_op jit(solution)/shard_map/all_to_all | solution.py:312
  69.2 5.8 %copy-start.2 = (bf16[16,2048,256]{2,1,0:T(8,128)(2,1)S(1)}, bf16[16,2048,256]{2,1,0:T(8,128)(2,1)}, u32[]{:S(2)}) copy-start(bf16[16,2048,256]{2,1,0:T(8,128)(2,1)} %copy-done) | copy-start | bytes 50331652
  74.9 1.2 %copy-start.17 = (bf16[2048,256]{1,0:T(8,128)(2,1)S(1)}, bf16[2048,256]{1,0:T(8,128)(2,1)}, u32[]{:S(2)}) copy-start(bf16[2048,256]{1,0:T(8,128)(2,1)} %copy-done.16) | copy-start | bytes 3145732
  82.9 3.3 %copy-start.3 = (bf16[2048,2048]{1,0:T(8,128)(2,1)}, bf16[2048,2048]{1,0:T(8,128)(2,1)S(1)}, u32[]{:S(2)}) copy-start(bf16[2048,2048]{1,0:T(8,128)(2,1)S(1)} %get-tuple-element.22.hot) | copy-start | bytes 25165828
  86.2 1.3 %copy-start.5 = (f32[2048,256]{1,0:T(8,128)}, f32[2048,256]{1,0:T(8,128)S(1)}, u32[]{:S(2)}) copy-start(f32[2048,256]{1,0:T(8,128)S(1)} %get-tuple-element.21.grads) | copy-start | bytes 6291460
  94.0 3.4 %copy-start.4 = (bf16[2048,2048]{1,0:T(8,128)(2,1)S(1)}, bf16[2048,2048]{1,0:T(8,128)(2,1)}, u32[]{:S(2)}) copy-start(bf16[2048,2048]{1,0:T(8,128)(2,1)} %copy-done.3) | copy-start | bytes 25165828
  97.4 1.6 %copy-start.6 = (f32[2048,256]{1,0:T(8,128)S(1)}, f32[2048,256]{1,0:T(8,128)}, u32[]{:S(2)}) copy-start(f32[2048,256]{1,0:T(8,128)} %copy-done.5) | copy-start | bytes 6291460

commit v2 on v1

v2 whole, which is shorter than its diff:
```python
import jax
import jax.numpy as jnp
from jax import lax
from jax.experimental import pallas as pl
from jax.experimental.pallas import tpu as pltpu
from jax.sharding import PartitionSpec as P

BF16 = jnp.bfloat16
F32 = jnp.float32
I32 = jnp.int32
NODES = 2048
WIDTH = 256
PEERS = 128
SLOTS = 16
FAN = 16
GROUPS = NODES // 16
LOCAL = 8
REMOTE = 8
VMEM = pl.BlockSpec(memory_space=pltpu.VMEM)
HBM = pl.BlockSpec(memory_space=pltpu.HBM)
DMA = pltpu.SemaphoreType.DMA
BLOCK = 256
BLOCKS = NODES // BLOCK
MESSAGE = 40
STEP = 512
STEPS = NODES // STEP
PIECE = 4
FINISH_PIECE = 4
NN = (((1,), (0,)), ((), ()))
NT = (((1,), (1,)), ((), ()))
TN = (((0,), (0,)), ((), ()))


def dot(a, b, dims=NN):
    return lax.dot_general(a, b, dims, preferred_element_type=F32)


def one_hot(keys, shape, axis):
    return jnp.where(keys == lax.broadcasted_iota(I32, shape, axis), F32(1), F32(0)).astype(BF16)


def hub_column(hub):
    shape = (8, 8)
    diagonal = lax.broadcasted_iota(I32, shape, 0) == lax.broadcasted_iota(I32, shape, 1)
    spread = jnp.where(diagonal, jnp.broadcast_to(hub, shape), 0).astype(F32)
    return jnp.sum(spread, axis=1, keepdims=True).astype(I32)


def in_hbm(*arrays):
    return [pltpu.with_memory_space_constraint(array, pltpu.HBM) for array in arrays]


def start(source, target, semaphore):
    copy = pltpu.make_async_copy(source, target, semaphore)
    copy.start()
    return copy


def rows_of(block):
    return pl.ds(block * BLOCK, BLOCK)


def pack_kernel(features_hbm, lists_hbm, hub_hbm, packed, features, lists, hub, hot, rows, sems):
    get_lists = start(lists_hbm, lists, sems.at[0])
    get_hub = start(hub_hbm, hub, sems.at[1])
    get_features = start(features_hbm, features, sems.at[2])
    get_lists.wait()
    by_peer = lists[...].astype(F32).T.astype(I32)
    for slot in range(8):
        hot[slot * PEERS : (slot + 1) * PEERS, :] = one_hot(
            by_peer[:, slot : slot + 1], (PEERS, NODES), 1
        )
    get_hub.wait()
    hub_rows = one_hot(hub_column(hub[...]), (8, NODES), 1)
    hot[8 * PEERS : 8 * PEERS + 16, :] = jnp.concatenate(
        [hub_rows, jnp.zeros((8, NODES), BF16)], axis=0
    )
    get_features.wait()
    picked = dot(hot[...], features[...])
    for slot in range(8):
        block = picked[slot * PEERS : (slot + 1) * PEERS]
        rows[0, pl.ds(slot, PEERS, stride=8), :] = block[:, :PEERS]
        rows[1, pl.ds(slot, PEERS, stride=8), :] = block[:, PEERS:]
    hubs = jnp.broadcast_to(picked[8 * PEERS : 8 * PEERS + 8][None], (PEERS, 8, WIDTH))
    bound = jnp.concatenate([rows[0], rows[1]], axis=1).reshape(PEERS, 8, WIDTH)
    packed[...] = jnp.concatenate([bound, hubs], axis=1).astype(BF16)


def pack(features, lists, hub):
    return pl.pallas_call(
        pack_kernel,
        out_shape=pltpu.HBM((PEERS, SLOTS, WIDTH), BF16),
        in_specs=[HBM] * 3,
        out_specs=VMEM,
        scratch_shapes=[
            pltpu.VMEM((NODES, WIDTH), BF16),
            pltpu.VMEM((8, PEERS), I32),
            pltpu.VMEM((1, 8), I32),
            pltpu.VMEM((8 * PEERS + 16, NODES), BF16),
            pltpu.VMEM((2, 8 * PEERS, PEERS), F32),
            DMA((3,)),
        ],
        compiler_params=pltpu.CompilerParams(vmem_limit_bytes=24 << 20),
        cost_estimate=pl.CostEstimate(
            flops=2 * 1040 * NODES * WIDTH, bytes_accessed=2 << 20, transcendentals=0
        ),
        name="pack",
    )(*in_hbm(features, lists, hub))


def flatten_lanes(values):
    k, n = values.shape
    per = 256 // k
    lane = lax.broadcasted_iota(I32, (k, 256), 1)
    own = lax.broadcasted_iota(I32, (k, 256), 0) == (lane & (k - 1))
    tiled = dot(values.astype(BF16), jnp.where(own, F32(1), F32(0)).astype(BF16), TN)
    shape = (n // per, per, 256)
    shift = k.bit_length() - 1
    mine = (lax.broadcasted_iota(I32, shape, 2) >> shift) == lax.broadcasted_iota(I32, shape, 1)
    return jnp.sum(jnp.where(mine, tiled.reshape(shape), F32(0)), axis=1)


CHUNK = 512
CHUNKS = NODES // CHUNK


def count_kernel(
    neighbours_hbm,
    counts_hbm,
    features_hbm,
    table_hbm,
    summed_hbm,
    neighbours,
    counts,
    features,
    table,
    summed,
    key_hi,
    key_lo,
    in_sems,
    table_sems,
    summed_sems,
):
    get_neighbours = start(neighbours_hbm, neighbours, in_sems.at[0])
    get_counts = start(counts_hbm, counts, in_sems.at[1])
    get_features = start(features_hbm, features, in_sems.at[2])
    get_neighbours.wait()
    index = neighbours[...]
    bound = index - NODES
    hub = bound - 8 * PEERS
    index = jnp.where(
        index < NODES,
        index,
        jnp.where(
            hub < 0,
            NODES + ((bound >> 3) << 4) + (bound & 7),
            NODES + ((hub >> 3) << 4) + 8 + (hub & 7),
        ),
    )
    get_counts.wait()
    usable = lax.broadcasted_iota(I32, index.shape, 0) < counts[...]
    index = jnp.where(usable, index, 4096)
    lane = lax.broadcasted_iota(I32, (GROUPS, 256), 1)
    key_hi[...] = flatten_lanes((index >> 8).astype(F32)) * 16.0 + (lane >> 4).astype(F32)
    key_lo[...] = flatten_lanes((index & 255).astype(F32))
    get_features.wait()

    def one_group(group, carry):
        rows = lax.broadcasted_iota(I32, (256, 256), 0).astype(F32).astype(BF16)
        hi = jnp.broadcast_to(key_hi[pl.ds(group, 1), :].astype(BF16), (256, 256))
        lo = jnp.broadcast_to(key_lo[pl.ds(group, 1), :].astype(BF16), (256, 256))
        left = jnp.where(hi == rows, BF16(1), BF16(0))
        right = jnp.where(lo == rows, BF16(1), BF16(0))
        block = dot(left, right, NT).astype(BF16)
        table[:, pl.ds(pl.multiple_of(group * 16, 16), 16), :] = block.reshape(16, 16, 256)
        return carry

    copies = []
    for chunk in range(CHUNKS):
        lax.fori_loop(
            chunk * CHUNK // 16, (chunk + 1) * CHUNK // 16, one_group, 0, unroll=16
        )
        at = pl.ds(chunk * CHUNK, CHUNK)
        copies.append(start(table.at[:, at], table_hbm.at[:, at], table_sems.at[chunk]))
        total = jnp.zeros((CHUNK, WIDTH), F32)
        for hi in range(LOCAL):
            total = total + dot(table[hi, at, :], features[hi * 256 : (hi + 1) * 256, :])
        summed[at, :] = total
        copies.append(start(summed.at[at], summed_hbm.at[at], summed_sems.at[chunk]))
    for copy in copies:
        copy.wait()


def count(neighbours, counts, features):
    return pl.pallas_call(
        count_kernel,
        out_shape=(
            pltpu.HBM((LOCAL + REMOTE, NODES, WIDTH), BF16),
            pltpu.HBM((NODES, WIDTH), F32),
        ),
        in_specs=[HBM] * 3,
        out_specs=[HBM] * 2,
        scratch_shapes=[
            pltpu.VMEM((FAN, NODES), I32),
            pltpu.VMEM((1, NODES), I32),
            pltpu.VMEM((NODES, WIDTH), BF16),
            pltpu.VMEM((LOCAL + REMOTE, NODES, WIDTH), BF16),
            pltpu.VMEM((NODES, WIDTH), F32),
            pltpu.VMEM((GROUPS, 256), F32),
            pltpu.VMEM((GROUPS, 256), F32),
            DMA((3,)),
            DMA((CHUNKS,)),
            DMA((CHUNKS,)),
        ],
        compiler_params=pltpu.CompilerParams(vmem_limit_bytes=40 << 20),
        cost_estimate=pl.CostEstimate(
            flops=2 * NODES * 4096 * WIDTH * 2, bytes_accessed=20 << 20, transcendentals=0
        ),
        name="count",
    )(*in_hbm(neighbours, counts, features))


def node_kernel(
    arrived,
    table_hbm,
    summed_hbm,
    features_hbm,
    counts_hbm,
    cotangent_hbm,
    self_weight_hbm,
    neighbour_weight_hbm,
    activations_hbm,
    grad_pre_hbm,
    edge_hbm,
    message_hbm,
    table,
    summed,
    features,
    counts,
    cotangent,
    self_weight,
    neighbour_weight,
    activations,
    grad_pre,
    edge,
    mean,
    message,
    weights,
    parts,
    small_sems,
    in_sems,
    out_sems,
    message_sems,
):
    get_small = [
        start(counts_hbm, counts, small_sems.at[0]),
        start(self_weight_hbm, self_weight, small_sems.at[1]),
        start(neighbour_weight_hbm, neighbour_weight, small_sems.at[2]),
    ]
    get = []
    for step in range(STEPS):
        at = pl.ds(step * STEP, STEP)
        get.append(
            [
                start(
                    table_hbm.at[pl.ds(LOCAL, REMOTE), at], table.at[:, at], in_sems.at[1, step]
                ),
                start(summed_hbm.at[at], summed.at[at], in_sems.at[2, step]),
                start(features_hbm.at[at], features.at[at], in_sems.at[0, step]),
                start(cotangent_hbm.at[at], cotangent.at[at], in_sems.at[3, step]),
            ]
        )
    for copy in get_small:
        copy.wait()
    inverse = (1.0 / counts[...].astype(F32)).T
    remote = arrived[...].reshape(NODES, WIDTH)
    scales = [
        jnp.concatenate(
            [
                jnp.broadcast_to(inverse[:, part : part + 1], (128, 256))
                for part in range(step * STEP // 128, (step + 1) * STEP // 128)
            ],
            axis=0,
        )
        for step in range(STEPS)
    ]

    def gather(step):
        for copy in get[step]:
            copy.wait()
        at = slice(step * STEP, (step + 1) * STEP)
        total = summed[at, :]
        for hi in range(REMOTE):
            total = total + dot(table[hi, at, :], remote[hi * 256 : (hi + 1) * 256])
        return (total * scales[step]).astype(BF16)

    def update(step, block_mean):
        at = slice(step * STEP, (step + 1) * STEP)
        mean[at, :] = block_mean
        pre = dot(features[at, :], self_weight[...]) + dot(block_mean, neighbour_weight[...])
        sigmoid = 0.5 * jnp.tanh(0.5 * pre) + 0.5
        activations[at, :] = (pre * sigmoid).astype(BF16)
        slope = sigmoid * (1.0 + pre * (1.0 - sigmoid))
        block_grad = (cotangent[at, :].astype(F32) * slope).astype(BF16)
        grad_pre[at, :] = block_grad
        edge[at, :] = (dot(block_grad, neighbour_weight[...], NT) * scales[step]).astype(BF16)

    now = gather(0)
    for step in range(STEPS):
        later = gather(step + 1) if step + 1 < STEPS else None
        update(step, now)
        now = later
    put = [
        start(activations, activations_hbm, out_sems.at[0]),
        start(grad_pre, grad_pre_hbm, out_sems.at[1]),
        start(edge, edge_hbm, out_sems.at[2]),
    ]
    for part, left in ((0, features), (1, mean)):
        product = dot(left[...], grad_pre[...], TN)
        weights[0, part * WIDTH : (part + 1) * WIDTH, :] = product[:, :128]
        weights[1, part * WIDTH : (part + 1) * WIDTH, :] = product[:, 128:]
    for half in range(2):
        for row in range(4):
            parts[pl.ds(half * 4 + row, PEERS, stride=8), :] = weights[
                half, pl.ds(row, PEERS, stride=4), :
            ]
    message[:, 32:40, :] = parts[...].reshape(PEERS, 8, 128).astype(BF16)
    for hi in range(REMOTE):
        added = dot(table[hi], edge[...], TN).astype(BF16).reshape(16, 16, WIDTH)
        message[hi * 16 : (hi + 1) * 16, 0:16, :] = added[:, :, :128]
        message[hi * 16 : (hi + 1) * 16, 16:32, :] = added[:, :, 128:]
        if (hi + 1) % PIECE == 0:
            peers = pl.ds((hi + 1 - PIECE) * 16, PIECE * 16)
            put.append(start(message.at[peers], message_hbm.at[peers], message_sems.at[hi]))
    for copy in put:
        copy.wait()


def node(
    arrived, table, summed, features, counts, cotangent, self_weight, neighbour_weight
):
    rows = pltpu.VMEM((NODES, WIDTH), BF16)
    return pl.pallas_call(
        node_kernel,
        out_shape=(
            pltpu.HBM((NODES, WIDTH), BF16),
            pltpu.HBM((NODES, WIDTH), BF16),
            pltpu.HBM((NODES, WIDTH), BF16),
            pltpu.HBM((PEERS, MESSAGE, 128), BF16),
        ),
        in_specs=[VMEM] + [HBM] * 7,
        out_specs=[HBM] * 4,
        scratch_shapes=[
            pltpu.VMEM((REMOTE, NODES, WIDTH), BF16),
            pltpu.VMEM((NODES, WIDTH), F32),
            rows,
            pltpu.VMEM((16, 128), I32),
            rows,
            pltpu.VMEM((WIDTH, WIDTH), BF16),
            pltpu.VMEM((WIDTH, WIDTH), BF16),
            rows,
            rows,
            rows,
            rows,
            pltpu.VMEM((PEERS, MESSAGE, 128), BF16),
            pltpu.VMEM((2, 2 * WIDTH, 128), F32),
            pltpu.VMEM((8 * PEERS, 128), F32),
            DMA((3,)),
            DMA((4, STEPS)),
            DMA((3,)),
            DMA((REMOTE,)),
        ],
        compiler_params=pltpu.CompilerParams(vmem_limit_bytes=40 << 20),
        cost_estimate=pl.CostEstimate(
            flops=2 * NODES * 2048 * WIDTH * 2, bytes_accessed=16 << 20, transcendentals=0
        ),
        name="node",
    )(
        arrived,
        *in_hbm(table, summed, features, counts, cotangent, self_weight, neighbour_weight),
    )


def local_kernel(
    table_hbm,
    edge_hbm,
    grad_pre_hbm,
    self_weight_hbm,
    lists_hbm,
    grads_hbm,
    ids,
    table,
    edge,
    grad_pre,
    self_weight,
    lists,
    grads,
    in_sems,
    table_sems,
    out_sems,
):
    get_edge = start(edge_hbm, edge, in_sems.at[0])
    get = [start(table_hbm.at[hi], table.at[hi], table_sems.at[hi]) for hi in range(LOCAL)]
    get_small = [
        start(grad_pre_hbm, grad_pre, in_sems.at[1]),
        start(self_weight_hbm, self_weight, in_sems.at[2]),
        start(lists_hbm, lists, in_sems.at[3]),
    ]
    for copy in get_small:
        copy.wait()
    ids[...] = flatten_lanes((lists[...] >> 8).astype(F32)) * 256.0 + flatten_lanes(
        (lists[...] & 255).astype(F32)
    )
    get_edge.wait()
    for copy in get:
        copy.wait()
    for hi in range(LOCAL):
        at = slice(hi * 256, (hi + 1) * 256)
        grads[at, :] = dot(table[hi], edge[...], TN) + dot(grad_pre[at, :], self_weight[...], NT)
    start(grads, grads_hbm, out_sems.at[0]).wait()


def local(table, edge, grad_pre, self_weight, lists):
    rows = pltpu.VMEM((NODES, WIDTH), BF16)
    return pl.pallas_call(
        local_kernel,
        out_shape=(
            pltpu.HBM((NODES, WIDTH), F32),
            pltpu.HBM((4, 256), F32),
        ),
        in_specs=[HBM] * 5,
        out_specs=[HBM, VMEM],
        scratch_shapes=[
            pltpu.VMEM((LOCAL, NODES, WIDTH), BF16),
            rows,
            rows,
            pltpu.VMEM((WIDTH, WIDTH), BF16),
            pltpu.VMEM((8, PEERS), I32),
            pltpu.VMEM((NODES, WIDTH), F32),
            DMA((4,)),
            DMA((LOCAL,)),
            DMA((1,)),
        ],
        compiler_params=pltpu.CompilerParams(vmem_limit_bytes=40 << 20),
        cost_estimate=pl.CostEstimate(
            flops=2 * NODES * 2048 * WIDTH, bytes_accessed=14 << 20, transcendentals=0
        ),
        name="local",
    )(*in_hbm(table, edge, grad_pre, self_weight, lists))


def finish_kernel(
    returned,
    grads_hbm,
    ids_hbm,
    hub_hbm,
    grad_features_hbm,
    grad_weights,
    grads,
    ids,
    hub,
    totals,
    sems,
    put_sems,
):
    get_ids = start(ids_hbm, ids, sems.at[0])
    get_hub = start(hub_hbm, hub, sems.at[1])
    get_grads = start(grads_hbm, grads, sems.at[2])
    sides = [returned[:, 0:16, :].astype(F32), returned[:, 16:32, :].astype(F32)]
    bound = jnp.concatenate([side[:, :8].reshape(8 * PEERS, 128) for side in sides], axis=1)
    bound = bound.astype(BF16)
    hubs = jnp.concatenate([jnp.sum(side[:, 8:], axis=0) for side in sides], axis=1)
    high = hubs.astype(BF16).astype(F32)
    hubs = jnp.concatenate([high, hubs - high], axis=0).astype(BF16)
    weights = jnp.sum(returned[:, 32:40, :].astype(F32), axis=0)
    grad_weights[...] = jnp.concatenate([weights[:4], weights[4:]], axis=1)
    get_ids.wait()
    get_hub.wait()
    get_grads.wait()
    put = []
    rows = lax.broadcasted_iota(I32, (BLOCK, 256), 0).astype(F32).astype(BF16)
    twice = jnp.concatenate([hub[...], hub[...]], axis=1)
    for block in range(BLOCKS):
        at = slice(block * BLOCK, (block + 1) * BLOCK)
        offset = ids[...] - block * 256.0
        inside = (offset >= 0.0) & (offset < 256.0)
        keys = jnp.where(inside, offset, -1.0).astype(BF16)
        hot = jnp.concatenate(
            [
                jnp.where(
                    jnp.broadcast_to(keys[part : part + 1, :], (BLOCK, 256)) == rows,
                    BF16(1),
                    BF16(0),
                )
                for part in range(4)
            ],
            axis=1,
        )
        hub_hot = one_hot(
            jnp.broadcast_to(twice - block * BLOCK, (BLOCK, 16)), (BLOCK, 16), 0
        )
        totals[at, :] = grads[at, :] + dot(hot, bound) + dot(hub_hot, hubs)
        if (block + 1) % FINISH_PIECE == 0:
            piece = pl.ds((block + 1 - FINISH_PIECE) * BLOCK, FINISH_PIECE * BLOCK)
            put.append(start(totals.at[piece], grad_features_hbm.at[piece], put_sems.at[block]))
    for copy in put:
        copy.wait()


def finish(returned, grads, ids, hub):
    return pl.pallas_call(
        finish_kernel,
        out_shape=(
            pltpu.HBM((NODES, WIDTH), F32),
            jax.ShapeDtypeStruct((4, WIDTH), F32),
        ),
        in_specs=[VMEM, HBM, HBM, HBM],
        out_specs=[HBM, VMEM],
        scratch_shapes=[
            pltpu.VMEM((NODES, WIDTH), F32),
            pltpu.VMEM((4, 256), F32),
            pltpu.VMEM((1, 8), I32),
            pltpu.VMEM((NODES, WIDTH), F32),
            DMA((3,)),
            DMA((BLOCKS,)),
        ],
        compiler_params=pltpu.CompilerParams(vmem_limit_bytes=32 << 20),
        cost_estimate=pl.CostEstimate(
            flops=2 * NODES * 1024 * WIDTH, bytes_accessed=6 << 20, transcendentals=0
        ),
        name="finish",
    )(returned, *in_hbm(grads, ids, hub))


def body(
    features, self_weight, neighbour_weight, send_lists, hub_nodes, neighbours, counts, cotangent
):
    lists = send_lists[0].T
    packed = pack(features, lists, hub_nodes)
    arrived = lax.all_to_all(packed, "dom", split_axis=0, concat_axis=0, tiled=True)
    table, summed = count(neighbours.T, counts.reshape(1, NODES), features)
    activations, grad_pre, edge, message = node(
        arrived,
        table,
        summed,
        features,
        counts.reshape(16, 128),
        cotangent,
        self_weight,
        neighbour_weight,
    )
    returned = lax.all_to_all(message, "dom", split_axis=0, concat_axis=0, tiled=True)
    grads, ids = local(table, edge, grad_pre, self_weight, lists)
    grad_features, grad_weights = finish(returned, grads, ids, hub_nodes)
    return (activations, grad_features, grad_weights)


def solution(mesh):
    in_specs = (
        P("dom", None),
        P(),
        P(),
        P("dom", None, None),
        P("dom", None),
        P("dom", None),
        P("dom"),
        P("dom", None),
    )
    out_specs = (P("dom", None), P("dom", None), P("dom", None))
    return jax.shard_map(body, mesh=mesh, in_specs=in_specs, out_specs=out_specs, check_vma=False)
```

time: 103 us -> 82.5 us (0.80)
  local copies, waits for them, and re-layouts: 40.4 us -> 0 us
  waiting for transfers between devices: 7.21 us -> 20.1 us
  Pallas kernels: 33.8 us -> 45.1 us
  starting transfers between devices: 20.6 us -> 16.1 us
    unnamed x52 -> x0, local copies, waits for them, and re-layouts: 40.4 us -> none
    pallas_call x5, Pallas kernels: 33.8 us -> 45.1 us  [the longest x1 14.6 us: node(): pl.pallas_call(node_kernel, out_shape=(pltpu.HBM((NODES, WIDTH), BF16), p...]
    all_to_all x1, waiting for transfers between devices: 6.5 us -> 13.5 us  [body(): lax.all_to_all(message, 'dom', split_axis=0, concat_axis=0, tiled=True)]
    all_to_all x1, waiting for transfers between devices: 0.71 us -> 6.6 us  [body(): lax.all_to_all(packed, 'dom', split_axis=0, concat_axis=0, tiled=True)]
    all_to_all x1, starting transfers between devices: 9.06 us -> 4.61 us  [body(): lax.all_to_all(message, 'dom', split_axis=0, concat_axis=0, tiled=True)]
  transfers between devices with their start and end apart: 2 -> 2, of which waited for: 2 -> 2; matrix products, arithmetic and copies ran while one was open for 0% -> 0% of each run, Pallas kernels for 17% -> 26%
where the time goes in v2:
time: 82.5 us; the launch traced here: 82.2 us
  Pallas kernels  45.1 us (55%)
  waiting for transfers between devices  20.1 us (24%)
  starting transfers between devices  16.1 us (20%)
  between operations  0.84 us (1%)
    pallas_call x1, Pallas kernels, node(): pl.pallas_call(node_kernel, out_shape=(pltpu.HBM((NODES, WIDTH), BF16), p...  14.6 us
    all_to_all x1, waiting for transfers between devices, body(): lax.all_to_all(message, 'dom', split_axis=0, concat_axis=0, tiled=True)  13.5 us
    pallas_call x1, Pallas kernels, count(): pl.pallas_call(count_kernel, out_shape=(pltpu.HBM((LOCAL + REMOTE, NODES,...  12.7 us
    all_to_all x1, starting transfers between devices, body(): lax.all_to_all(packed, 'dom', split_axis=0, concat_axis=0, tiled=True)  11.5 us
    pallas_call x1, Pallas kernels, local(): pl.pallas_call(local_kernel, out_shape=(pltpu.HBM((NODES, WIDTH), F32), p...  8.74 us
    all_to_all x1, waiting for transfers between devices, body(): lax.all_to_all(packed, 'dom', split_axis=0, concat_axis=0, tiled=True)  6.6 us
    pallas_call x1, Pallas kernels, finish(): pl.pallas_call(finish_kernel, out_shape=(pltpu.HBM((NODES, WIDTH), F32),...  4.8 us
    all_to_all x1, starting transfers between devices, body(): lax.all_to_all(message, 'dom', split_axis=0, concat_axis=0, tiled=True)  4.61 us
  transfers between devices with their start and end apart: 2, of which 2 were waited for; matrix products, arithmetic and copies ran while one was open for 0% of the time, Pallas kernels for 26%

profile of v2, /device:TPU:1, one launch (start us, length us, event | category | flops | bytes accessed | tf_op | source)
XLA Modules:
  0.0 82.2 jit_solution(4771493397124797618)
XLA Ops:
  0.6 4.3 %pack.1 = bf16[128,16,256]{2,1,0:T(8,128)(2,1)} custom-call(bf16[2048,256]{1,0:T(8,128)(2,1)} %features_hbm.5, s32[8,128]{1,0:T(8,128)} %bitcast.8, s32[1,8]{1,0:T(1,128)} %hub_hbm.3), custom_call_target="tpu_custom_call" | custom-call | flops 1090519040 | bytes 2097152 | tf_op jit(solution)/shard_map/pack/pallas_call | solution.py:90
  5.0 11.5 %all-to-all-start = ((bf16[128,16,256]{2,1,0:T(8,128)(2,1)}), bf16[128,16,256]{2,1,0:T(8,128)(2,1)S(1)}, u32[]{:S(2)}, u32[]{:S(2)}) async-start(bf16[128,16,256]{2,1,0:T(8,128)(2,1)} %pack.1), calls=%async_computation | async-start | bytes 2097152 | tf_op jit(solution)/shard_map/all_to_all | solution.py:540
  16.5 12.7 %count.1 = (bf16[16,2048,256]{2,1,0:T(8,128)(2,1)}, f32[2048,256]{1,0:T(8,128)}) custom-call(s32[16,2048]{1,0:T(8,128)} %bitcast.10, s32[1,2048]{1,0:T(1,128)} %bitcast.6, bf16[2048,256]{1,0:T(8,128)(2,1)} %features_hbm.5), custom_call_target="tpu_custom_call" | custom-call | flops 8589934592 | bytes 20971520 | tf_op jit(solution)/shard_map/count/pallas_call | solution.py:195
  29.2 6.6 %all-to-all-done.arrived = bf16[128,16,256]{2,1,0:T(8,128)(2,1)S(1)} async-done(((bf16[128,16,256]{2,1,0:T(8,128)(2,1)}), bf16[128,16,256]{2,1,0:T(8,128)(2,1)S(1)}, u32[]{:S(2)}, u32[]{:S(2)}) %all-to-all-start) | async-done | bytes 1048608 | tf_op jit(solution)/shard_map/all_to_all | solution.py:540
  35.8 14.6 %node.1 = (bf16[2048,256]{1,0:T(8,128)(2,1)}, bf16[2048,256]{1,0:T(8,128)(2,1)}, bf16[2048,256]{1,0:T(8,128)(2,1)}, bf16[128,40,128]{2,1,0:T(8,128)(2,1)}) custom-call(bf16[128,16,256]{2,1,0:T(8,128)(2,1)S(1)} %all-to-all-done.arrived, bf16[16,2048,256]{2,1,0:T(8,128)(2,1)} %get-tuple-element.13.table_hbm, f32[2048,256]{1,0:T(8,128)} %get-tuple-element.14.summed_hbm, ...), custom_call_target="tpu_custom_call" | custom-call | flops 4294967296 | bytes 16777216 | tf_op jit(solution)/shard_map/node/pallas_call | solution.py:343
  50.4 4.6 %all-to-all-start.1 = ((bf16[128,40,128]{2,1,0:T(8,128)(2,1)}), bf16[128,40,128]{2,1,0:T(8,128)(2,1)S(1)}, u32[]{:S(2)}, u32[]{:S(2)}) async-start(bf16[128,40,128]{2,1,0:T(8,128)(2,1)} %get-tuple-element.16), calls=%async_computation.1 | async-start | bytes 2621440 | tf_op jit(solution)/shard_map/all_to_all | solution.py:552
  55.0 8.7 %local.1 = (f32[2048,256]{1,0:T(8,128)}, f32[4,256]{1,0:T(4,128)}) custom-call(bf16[16,2048,256]{2,1,0:T(8,128)(2,1)} %get-tuple-element.13.table_hbm, bf16[2048,256]{1,0:T(8,128)(2,1)} %get-tuple-element.17.edge_hbm, bf16[2048,256]{1,0:T(8,128)(2,1)} %get-tuple-element.18.grad_pre_hbm, bf16[256,256]{1,0:T(8,128)(2,1)} %self_weight_hbm.3, s32[8,128]{1,0:T(8,128)} %bitcast.9), custom_call_target="tpu_custom_call" | custom-call | flops 2147483648 | bytes 14680064 | tf_op jit(solution)/shard_map/local/pallas_call | solution.py:425
  63.7 13.5 %all-to-all-done.1.returned = bf16[128,40,128]{2,1,0:T(8,128)(2,1)S(1)} async-done(((bf16[128,40,128]{2,1,0:T(8,128)(2,1)}), bf16[128,40,128]{2,1,0:T(8,128)(2,1)S(1)}, u32[]{:S(2)}, u32[]{:S(2)}) %all-to-all-start.1) | async-done | bytes 1310752 | tf_op jit(solution)/shard_map/all_to_all | solution.py:552
  77.2 4.8 %finish.1 = (f32[2048,256]{1,0:T(8,128)}, f32[4,256]{1,0:T(4,128)}) custom-call(bf16[128,40,128]{2,1,0:T(8,128)(2,1)S(1)} %all-to-all-done.1.returned, f32[2048,256]{1,0:T(8,128)} %get-tuple-element.19.grads_hbm, f32[4,256]{1,0:T(4,128)} %get-tuple-element.20.ids_hbm, s32[1,8]{1,0:T(1,128)} %hub_hbm.3), custom_call_target="tpu_custom_call" | custom-call | flops 1073741824 | bytes 6291456 | tf_op jit(solution)/shard_map/finish/pallas_call | solution.py:511
Async XLA Ops:
  5.0 30.8 %all-to-all-start = ((bf16[128,16,256]{2,1,0:T(8,128)(2,1)}), bf16[128,16,256]{2,1,0:T(8,128)(2,1)S(1)}, u32[]{:S(2)}, u32[]{:S(2)}) async-start(bf16[128,16,256]{2,1,0:T(8,128)(2,1)} %pack.1), calls=%async_computation | async-start | bytes 2097152 | tf_op jit(solution)/shard_map/all_to_all | solution.py:540
  50.4 26.8 %all-to-all-start.1 = ((bf16[128,40,128]{2,1,0:T(8,128)(2,1)}), bf16[128,40,128]{2,1,0:T(8,128)(2,1)S(1)}, u32[]{:S(2)}, u32[]{:S(2)}) async-start(bf16[128,40,128]{2,1,0:T(8,128)(2,1)} %get-tuple-element.16), calls=%async_computation.1 | async-start | bytes 2621440 | tf_op jit(solution)/shard_map/all_to_all | solution.py:552

commit v3 on v2

--- a/solution.py
+++ b/solution.py
@@ -6,6 +6,9 @@
 from jax.sharding import PartitionSpec as P
 
 BF16 = jnp.bfloat16
+COUNT = jnp.float8_e4m3fn
+PRODUCT = jnp.float8_e4m3fn
+UNROLL = 16
 F32 = jnp.float32
 I32 = jnp.int32
 NODES = 2048
@@ -25,7 +28,7 @@
 STEP = 512
 STEPS = NODES // STEP
 PIECE = 4
-FINISH_PIECE = 4
+FINISH_PIECE = 2
 NN = (((1,), (0,)), ((), ()))
 NT = (((1,), (1,)), ((), ()))
 TN = (((0,), (0,)), ((), ()))
@@ -50,9 +53,9 @@
     return [pltpu.with_memory_space_constraint(array, pltpu.HBM) for array in arrays]
 
 
-def start(source, target, semaphore):
+def start(source, target, semaphore, priority=0):
     copy = pltpu.make_async_copy(source, target, semaphore)
-    copy.start()
+    copy.start(priority=priority)
     return copy
 
 
@@ -60,23 +63,23 @@
     return pl.ds(block * BLOCK, BLOCK)
 
 
-def pack_kernel(features_hbm, lists_hbm, hub_hbm, packed, features, lists, hub, hot, rows, sems):
+def pack_kernel(features_hbm, lists_hbm, hub_hbm, packed, features, lists, hub, rows, sems):
     get_lists = start(lists_hbm, lists, sems.at[0])
     get_hub = start(hub_hbm, hub, sems.at[1])
     get_features = start(features_hbm, features, sems.at[2])
     get_lists.wait()
+    get_hub.wait()
+    get_features.wait()
     by_peer = lists[...].astype(F32).T.astype(I32)
-    for slot in range(8):
-        hot[slot * PEERS : (slot + 1) * PEERS, :] = one_hot(
-            by_peer[:, slot : slot + 1], (PEERS, NODES), 1
-        )
-    get_hub.wait()
-    hub_rows = one_hot(hub_column(hub[...]), (8, NODES), 1)
-    hot[8 * PEERS : 8 * PEERS + 16, :] = jnp.concatenate(
-        [hub_rows, jnp.zeros((8, NODES), BF16)], axis=0
+    none = jnp.full((8, 1), -1, I32)
+    column = jnp.concatenate(
+        [by_peer[:, slot : slot + 1] for slot in range(8)] + [hub_column(hub[...]), none], axis=0
     )
-    get_features.wait()
-    picked = dot(hot[...], features[...])
+    shape = (8 * PEERS + 16, 256)
+    picked = jnp.zeros(shape, F32)
+    for chunk in range(8):
+        hot = one_hot(jnp.broadcast_to(column - chunk * 256, shape), shape, 1)
+        picked = picked + dot(hot, features[chunk * 256 : (chunk + 1) * 256, :])
     for slot in range(8):
         block = picked[slot * PEERS : (slot + 1) * PEERS]
         rows[0, pl.ds(slot, PEERS, stride=8), :] = block[:, :PEERS]
@@ -96,7 +99,6 @@
             pltpu.VMEM((NODES, WIDTH), BF16),
             pltpu.VMEM((8, PEERS), I32),
             pltpu.VMEM((1, 8), I32),
-            pltpu.VMEM((8 * PEERS + 16, NODES), BF16),
             pltpu.VMEM((2, 8 * PEERS, PEERS), F32),
             DMA((3,)),
         ],
@@ -165,28 +167,39 @@
     key_lo[...] = flatten_lanes((index & 255).astype(F32))
     get_features.wait()
 
-    def one_group(group, carry):
-        rows = lax.broadcasted_iota(I32, (256, 256), 0).astype(F32).astype(BF16)
+    rows = lax.broadcasted_iota(I32, (256, 256), 0).astype(F32).astype(BF16)
+
+    def products(group):
         hi = jnp.broadcast_to(key_hi[pl.ds(group, 1), :].astype(BF16), (256, 256))
         lo = jnp.broadcast_to(key_lo[pl.ds(group, 1), :].astype(BF16), (256, 256))
-        left = jnp.where(hi == rows, BF16(1), BF16(0))
-        right = jnp.where(lo == rows, BF16(1), BF16(0))
-        block = dot(left, right, NT).astype(BF16)
-        table[:, pl.ds(pl.multiple_of(group * 16, 16), 16), :] = block.reshape(16, 16, 256)
+        left = jnp.where(hi == rows, BF16(1), BF16(0)).astype(PRODUCT)
+        right = jnp.where(lo == rows, BF16(1), BF16(0)).astype(PRODUCT)
+        return dot(left, right, NT).reshape(16, 16, 256)
+
+    def one_pair(pair, carry):
+        both = jnp.concatenate([products(2 * pair), products(2 * pair + 1)], axis=1)
+        at = pl.ds(pl.multiple_of(pair * 32, 32), 32)
+        table[:, at, :] = both.astype(COUNT)
         return carry
 
     copies = []
     for chunk in range(CHUNKS):
         lax.fori_loop(
-            chunk * CHUNK // 16, (chunk + 1) * CHUNK // 16, one_group, 0, unroll=16
+            chunk * CHUNK // 32, (chunk + 1) * CHUNK // 32, one_pair, 0, unroll=UNROLL
         )
         at = pl.ds(chunk * CHUNK, CHUNK)
         copies.append(start(table.at[:, at], table_hbm.at[:, at], table_sems.at[chunk]))
-        total = jnp.zeros((CHUNK, WIDTH), F32)
-        for hi in range(LOCAL):
-            total = total + dot(table[hi, at, :], features[hi * 256 : (hi + 1) * 256, :])
-        summed[at, :] = total
-        copies.append(start(summed.at[at], summed_hbm.at[at], summed_sems.at[chunk]))
+    for half in range(2):
+        for block in range(2 * half, 2 * half + 2):
+            at = slice(block * 512, (block + 1) * 512)
+            total = jnp.zeros((512, WIDTH), F32)
+            for hi in range(LOCAL):
+                total = total + dot(
+                    table[hi, at, :].astype(BF16), features[hi * 256 : (hi + 1) * 256, :]
+                )
+            summed[at, :] = total
+        at = pl.ds(half * 1024, 1024)
+        copies.append(start(summed.at[at], summed_hbm.at[at], summed_sems.at[half]))
     for copy in copies:
         copy.wait()
 
@@ -195,7 +208,7 @@
     return pl.pallas_call(
         count_kernel,
         out_shape=(
-            pltpu.HBM((LOCAL + REMOTE, NODES, WIDTH), BF16),
+            pltpu.HBM((LOCAL + REMOTE, NODES, WIDTH), COUNT),
             pltpu.HBM((NODES, WIDTH), F32),
         ),
         in_specs=[HBM] * 3,
@@ -204,7 +217,7 @@
             pltpu.VMEM((FAN, NODES), I32),
             pltpu.VMEM((1, NODES), I32),
             pltpu.VMEM((NODES, WIDTH), BF16),
-            pltpu.VMEM((LOCAL + REMOTE, NODES, WIDTH), BF16),
+            pltpu.VMEM((LOCAL + REMOTE, NODES, WIDTH), COUNT),
             pltpu.VMEM((NODES, WIDTH), F32),
             pltpu.VMEM((GROUPS, 256), F32),
             pltpu.VMEM((GROUPS, 256), F32),
@@ -260,14 +273,18 @@
     get = []
     for step in range(STEPS):
         at = pl.ds(step * STEP, STEP)
+        late = min(step, 1)
         get.append(
             [
                 start(
-                    table_hbm.at[pl.ds(LOCAL, REMOTE), at], table.at[:, at], in_sems.at[1, step]
+                    table_hbm.at[pl.ds(LOCAL, REMOTE), at],
+                    table.at[:, at],
+                    in_sems.at[1, step],
+                    late,
                 ),
-                start(summed_hbm.at[at], summed.at[at], in_sems.at[2, step]),
-                start(features_hbm.at[at], features.at[at], in_sems.at[0, step]),
-                start(cotangent_hbm.at[at], cotangent.at[at], in_sems.at[3, step]),
+                start(summed_hbm.at[at], summed.at[at], in_sems.at[2, step], late),
+                start(features_hbm.at[at], features.at[at], in_sems.at[0, step], late),
+                start(cotangent_hbm.at[at], cotangent.at[at], in_sems.at[3, step], late),
             ]
         )
     for copy in get_small:
@@ -291,7 +308,7 @@
         at = slice(step * STEP, (step + 1) * STEP)
         total = summed[at, :]
         for hi in range(REMOTE):
-            total = total + dot(table[hi, at, :], remote[hi * 256 : (hi + 1) * 256])
+            total = total + dot(table[hi, at, :].astype(BF16), remote[hi * 256 : (hi + 1) * 256])
         return (total * scales[step]).astype(BF16)
 
     def update(step, block_mean):
@@ -326,7 +343,7 @@
             ]
     message[:, 32:40, :] = parts[...].reshape(PEERS, 8, 128).astype(BF16)
     for hi in range(REMOTE):
-        added = dot(table[hi], edge[...], TN).astype(BF16).reshape(16, 16, WIDTH)
+        added = dot(table[hi].astype(BF16), edge[...], TN).astype(BF16).reshape(16, 16, WIDTH)
         message[hi * 16 : (hi + 1) * 16, 0:16, :] = added[:, :, :128]
         message[hi * 16 : (hi + 1) * 16, 16:32, :] = added[:, :, 128:]
         if (hi + 1) % PIECE == 0:
@@ -351,7 +368,7 @@
         in_specs=[VMEM] + [HBM] * 7,
         out_specs=[HBM] * 4,
         scratch_shapes=[
-            pltpu.VMEM((REMOTE, NODES, WIDTH), BF16),
+            pltpu.VMEM((REMOTE, NODES, WIDTH), COUNT),
             pltpu.VMEM((NODES, WIDTH), F32),
             rows,
             pltpu.VMEM((16, 128), I32),
@@ -416,7 +433,7 @@
         copy.wait()
     for hi in range(LOCAL):
         at = slice(hi * 256, (hi + 1) * 256)
-        grads[at, :] = dot(table[hi], edge[...], TN) + dot(grad_pre[at, :], self_weight[...], NT)
+        grads[at, :] = dot(table[hi].astype(BF16), edge[...], TN) + dot(grad_pre[at, :], self_weight[...], NT)
     start(grads, grads_hbm, out_sems.at[0]).wait()
 
 
@@ -431,7 +448,7 @@
         in_specs=[HBM] * 5,
         out_specs=[HBM, VMEM],
         scratch_shapes=[
-            pltpu.VMEM((LOCAL, NODES, WIDTH), BF16),
+            pltpu.VMEM((LOCAL, NODES, WIDTH), COUNT),
             rows,
             rows,
             pltpu.VMEM((WIDTH, WIDTH), BF16),

time: 82.5 us -> 79.7 us (0.966)
  Pallas kernels: 45.1 us -> 37.8 us
  waiting for transfers between devices: 20.1 us -> 24.4 us
    pallas_call x1, Pallas kernels: 12.7 us -> 9.25 us  [count(): pl.pallas_call(count_kernel, out_shape=(pltpu.HBM((LOCAL + REMOTE, NODES,...]
    all_to_all x1, waiting for transfers between devices: 6.6 us -> 9.83 us  [body(): lax.all_to_all(packed, 'dom', split_axis=0, concat_axis=0, tiled=True)]
    pallas_call x1, Pallas kernels: 14.6 us -> 11.9 us  [node(): pl.pallas_call(node_kernel, out_shape=(pltpu.HBM((NODES, WIDTH), BF16), p...]
    pallas_call x1, Pallas kernels: 8.74 us -> 7.63 us  [local(): pl.pallas_call(local_kernel, out_shape=(pltpu.HBM((NODES, WIDTH), F32), p...]
    all_to_all x1, waiting for transfers between devices: 13.5 us -> 14.6 us  [body(): lax.all_to_all(message, 'dom', split_axis=0, concat_axis=0, tiled=True)]
  transfers between devices with their start and end apart: 2 -> 2, of which waited for: 2 -> 2; matrix products, arithmetic and copies ran while one was open for 0% -> 0% of each run, Pallas kernels for 26% -> 21%
where the time goes in v3:
time: 79.7 us; the launch traced here: 79.3 us
  Pallas kernels  37.8 us (47%)
  waiting for transfers between devices  24.4 us (31%)
  starting transfers between devices  16.3 us (20%)
  between operations  0.86 us (1%)
    all_to_all x1, waiting for transfers between devices, body(): lax.all_to_all(message, 'dom', split_axis=0, concat_axis=0, tiled=True)  14.6 us
    pallas_call x1, Pallas kernels, node(): pl.pallas_call(node_kernel, out_shape=(pltpu.HBM((NODES, WIDTH), BF16), p...  11.9 us
    all_to_all x1, starting transfers between devices, body(): lax.all_to_all(packed, 'dom', split_axis=0, concat_axis=0, tiled=True)  11.7 us
    all_to_all x1, waiting for transfers between devices, body(): lax.all_to_all(packed, 'dom', split_axis=0, concat_axis=0, tiled=True)  9.83 us
    pallas_call x1, Pallas kernels, count(): pl.pallas_call(count_kernel, out_shape=(pltpu.HBM((LOCAL + REMOTE, NODES,...  9.25 us
    pallas_call x1, Pallas kernels, local(): pl.pallas_call(local_kernel, out_shape=(pltpu.HBM((NODES, WIDTH), F32), p...  7.63 us
    pallas_call x1, Pallas kernels, finish(): pl.pallas_call(finish_kernel, out_shape=(pltpu.HBM((NODES, WIDTH), F32),...  4.63 us
    all_to_all x1, starting transfers between devices, body(): lax.all_to_all(message, 'dom', split_axis=0, concat_axis=0, tiled=True)  4.61 us
  transfers between devices with their start and end apart: 2, of which 2 were waited for; matrix products, arithmetic and copies ran while one was open for 0% of the time, Pallas kernels for 21%

profile of v3, /device:TPU:1, one launch (start us, length us, event | category | flops | bytes accessed | tf_op | source)
XLA Modules:
  0.0 79.3 jit_solution(8436598676523743188)
XLA Ops:
  0.6 4.4 %pack.1 = bf16[128,16,256]{2,1,0:T(8,128)(2,1)} custom-call(bf16[2048,256]{1,0:T(8,128)(2,1)} %features_hbm.5, s32[8,128]{1,0:T(8,128)} %bitcast.6, s32[1,8]{1,0:T(1,128)} %hub_hbm.3), custom_call_target="tpu_custom_call" | custom-call | flops 1090519040 | bytes 2097152 | tf_op jit(solution)/shard_map/pack/pallas_call | solution.py:93
  5.0 11.7 %all-to-all-start = ((bf16[128,16,256]{2,1,0:T(8,128)(2,1)}), bf16[128,16,256]{2,1,0:T(8,128)(2,1)S(1)}, u32[]{:S(2)}, u32[]{:S(2)}) async-start(bf16[128,16,256]{2,1,0:T(8,128)(2,1)} %pack.1), calls=%async_computation | async-start | bytes 2097152 | tf_op jit(solution)/shard_map/all_to_all | solution.py:557
  16.7 9.3 %count.1 = (f8e4m3fn[16,2048,256]{2,1,0:T(32,128)(4,1)}, f32[2048,256]{1,0:T(8,128)}) custom-call(s32[16,2048]{1,0:T(8,128)} %bitcast.8, s32[1,2048]{1,0:T(1,128)} %bitcast.9, bf16[2048,256]{1,0:T(8,128)(2,1)} %features_hbm.5), custom_call_target="tpu_custom_call" | custom-call | flops 8589934592 | bytes 20971520 | tf_op jit(solution)/shard_map/count/pallas_call | solution.py:208
  26.0 9.8 %all-to-all-done.arrived = bf16[128,16,256]{2,1,0:T(8,128)(2,1)S(1)} async-done(((bf16[128,16,256]{2,1,0:T(8,128)(2,1)}), bf16[128,16,256]{2,1,0:T(8,128)(2,1)S(1)}, u32[]{:S(2)}, u32[]{:S(2)}) %all-to-all-start) | async-done | bytes 1048608 | tf_op jit(solution)/shard_map/all_to_all | solution.py:557
  35.8 11.9 %node.1 = (bf16[2048,256]{1,0:T(8,128)(2,1)}, bf16[2048,256]{1,0:T(8,128)(2,1)}, bf16[2048,256]{1,0:T(8,128)(2,1)}, bf16[128,40,128]{2,1,0:T(8,128)(2,1)}) custom-call(bf16[128,16,256]{2,1,0:T(8,128)(2,1)S(1)} %all-to-all-done.arrived, f8e4m3fn[16,2048,256]{2,1,0:T(32,128)(4,1)} %get-tuple-element.13.table_hbm, f32[2048,256]{1,0:T(8,128)} %get-tuple-element.14.summed_hbm, ...), custom_call_target="tpu_custom_call" | custom-call | flops 4294967296 | bytes 16777216 | tf_op jit(solution)/shard_map/node/pallas_call | solution.py:360
  47.7 4.6 %all-to-all-start.1 = ((bf16[128,40,128]{2,1,0:T(8,128)(2,1)}), bf16[128,40,128]{2,1,0:T(8,128)(2,1)S(1)}, u32[]{:S(2)}, u32[]{:S(2)}) async-start(bf16[128,40,128]{2,1,0:T(8,128)(2,1)} %get-tuple-element.16), calls=%async_computation.1 | async-start | bytes 2621440 | tf_op jit(solution)/shard_map/all_to_all | solution.py:569
  52.3 7.6 %local.1 = (f32[2048,256]{1,0:T(8,128)}, f32[4,256]{1,0:T(4,128)}) custom-call(f8e4m3fn[16,2048,256]{2,1,0:T(32,128)(4,1)} %get-tuple-element.13.table_hbm, bf16[2048,256]{1,0:T(8,128)(2,1)} %get-tuple-element.17.edge_hbm, bf16[2048,256]{1,0:T(8,128)(2,1)} %get-tuple-element.18.grad_pre_hbm, bf16[256,256]{1,0:T(8,128)(2,1)} %self_weight_hbm.3, s32[8,128]{1,0:T(8,128)} %bitcast.7), custom_call_target="tpu_custom_call" | custom-call | flops 2147483648 | bytes 14680064 | tf_op jit(solution)/shard_map/local/pallas_call | solution.py:442
  59.9 14.6 %all-to-all-done.1.returned = bf16[128,40,128]{2,1,0:T(8,128)(2,1)S(1)} async-done(((bf16[128,40,128]{2,1,0:T(8,128)(2,1)}), bf16[128,40,128]{2,1,0:T(8,128)(2,1)S(1)}, u32[]{:S(2)}, u32[]{:S(2)}) %all-to-all-start.1) | async-done | bytes 1310752 | tf_op jit(solution)/shard_map/all_to_all | solution.py:569
  74.5 4.6 %finish.1 = (f32[2048,256]{1,0:T(8,128)}, f32[4,256]{1,0:T(4,128)}) custom-call(bf16[128,40,128]{2,1,0:T(8,128)(2,1)S(1)} %all-to-all-done.1.returned, f32[2048,256]{1,0:T(8,128)} %get-tuple-element.19.grads_hbm, f32[4,256]{1,0:T(4,128)} %get-tuple-element.20.ids_hbm, s32[1,8]{1,0:T(1,128)} %hub_hbm.3), custom_call_target="tpu_custom_call" | custom-call | flops 1073741824 | bytes 6291456 | tf_op jit(solution)/shard_map/finish/pallas_call | solution.py:528
Async XLA Ops:
  5.0 30.8 %all-to-all-start = ((bf16[128,16,256]{2,1,0:T(8,128)(2,1)}), bf16[128,16,256]{2,1,0:T(8,128)(2,1)S(1)}, u32[]{:S(2)}, u32[]{:S(2)}) async-start(bf16[128,16,256]{2,1,0:T(8,128)(2,1)} %pack.1), calls=%async_computation | async-start | bytes 2097152 | tf_op jit(solution)/shard_map/all_to_all | solution.py:557
  47.7 26.8 %all-to-all-start.1 = ((bf16[128,40,128]{2,1,0:T(8,128)(2,1)}), bf16[128,40,128]{2,1,0:T(8,128)(2,1)S(1)}, u32[]{:S(2)}, u32[]{:S(2)}) async-start(bf16[128,40,128]{2,1,0:T(8,128)(2,1)} %get-tuple-element.16), calls=%async_computation.1 | async-start | bytes 2621440 | tf_op jit(solution)/shard_map/all_to_all | solution.py:569

commit v4 on v3

--- a/solution.py
+++ b/solution.py
@@ -25,8 +25,8 @@
 BLOCK = 256
 BLOCKS = NODES // BLOCK
 MESSAGE = 40
-STEP = 512
-STEPS = NODES // STEP
+CUTS = (0, 256, 768, 1280, 2048)
+STEPS = len(CUTS) - 1
 PIECE = 4
 FINISH_PIECE = 2
 NN = (((1,), (0,)), ((), ()))
@@ -42,13 +42,6 @@
     return jnp.where(keys == lax.broadcasted_iota(I32, shape, axis), F32(1), F32(0)).astype(BF16)
 
 
-def hub_column(hub):
-    shape = (8, 8)
-    diagonal = lax.broadcasted_iota(I32, shape, 0) == lax.broadcasted_iota(I32, shape, 1)
-    spread = jnp.where(diagonal, jnp.broadcast_to(hub, shape), 0).astype(F32)
-    return jnp.sum(spread, axis=1, keepdims=True).astype(I32)
-
-
 def in_hbm(*arrays):
     return [pltpu.with_memory_space_constraint(array, pltpu.HBM) for array in arrays]
 
@@ -63,29 +56,40 @@
     return pl.ds(block * BLOCK, BLOCK)
 
 
-def pack_kernel(features_hbm, lists_hbm, hub_hbm, packed, features, lists, hub, rows, sems):
+def flatten_lanes(values):
+    k, n = values.shape
+    per = 256 // k
+    lane = lax.broadcasted_iota(I32, (k, 256), 1)
+    own = lax.broadcasted_iota(I32, (k, 256), 0) == (lane & (k - 1))
+    tiled = dot(values.astype(BF16), jnp.where(own, F32(1), F32(0)).astype(BF16), TN)
+    shape = (n // per, per, 256)
+    shift = k.bit_length() - 1
+    mine = (lax.broadcasted_iota(I32, shape, 2) >> shift) == lax.broadcasted_iota(I32, shape, 1)
+    return jnp.sum(jnp.where(mine, tiled.reshape(shape), F32(0)), axis=1)
+
+
+def pack_kernel(features_hbm, lists_hbm, hub_hbm, packed, features, lists, hub, sems):
     get_lists = start(lists_hbm, lists, sems.at[0])
     get_hub = start(hub_hbm, hub, sems.at[1])
     get_features = start(features_hbm, features, sems.at[2])
     get_lists.wait()
     get_hub.wait()
     get_features.wait()
-    by_peer = lists[...].astype(F32).T.astype(I32)
-    none = jnp.full((8, 1), -1, I32)
-    column = jnp.concatenate(
-        [by_peer[:, slot : slot + 1] for slot in range(8)] + [hub_column(hub[...]), none], axis=0
+    ids = flatten_lanes((lists[...] >> 8).astype(F32)) * 256.0 + flatten_lanes(
+        (lists[...] & 255).astype(F32)
     )
-    shape = (8 * PEERS + 16, 256)
-    picked = jnp.zeros(shape, F32)
+    hub_ids = jnp.concatenate([hub[...].astype(F32), jnp.full((1, 120), -1.0, F32)], axis=1)
+    ids = jnp.concatenate([ids[part : part + 1] for part in range(4)] + [hub_ids], axis=1)
+    rows = lax.broadcasted_iota(I32, (256, 1152), 0).astype(F32).astype(BF16)
+    picked = jnp.zeros((1152, WIDTH), F32)
     for chunk in range(8):
-        hot = one_hot(jnp.broadcast_to(column - chunk * 256, shape), shape, 1)
-        picked = picked + dot(hot, features[chunk * 256 : (chunk + 1) * 256, :])
-    for slot in range(8):
-        block = picked[slot * PEERS : (slot + 1) * PEERS]
-        rows[0, pl.ds(slot, PEERS, stride=8), :] = block[:, :PEERS]
-        rows[1, pl.ds(slot, PEERS, stride=8), :] = block[:, PEERS:]
+        offset = ids - chunk * 256.0
+        inside = (offset >= 0.0) & (offset < 256.0)
+        keys = jnp.where(inside, offset, -1.0).astype(BF16)
+        hot = jnp.where(jnp.broadcast_to(keys, (256, 1152)) == rows, BF16(1), BF16(0))
+        picked = picked + dot(hot, features[chunk * 256 : (chunk + 1) * 256, :], TN)
     hubs = jnp.broadcast_to(picked[8 * PEERS : 8 * PEERS + 8][None], (PEERS, 8, WIDTH))
-    bound = jnp.concatenate([rows[0], rows[1]], axis=1).reshape(PEERS, 8, WIDTH)
+    bound = picked[: 8 * PEERS].reshape(PEERS, 8, WIDTH)
     packed[...] = jnp.concatenate([bound, hubs], axis=1).astype(BF16)
 
 
@@ -99,7 +103,6 @@
             pltpu.VMEM((NODES, WIDTH), BF16),
             pltpu.VMEM((8, PEERS), I32),
             pltpu.VMEM((1, 8), I32),
-            pltpu.VMEM((2, 8 * PEERS, PEERS), F32),
             DMA((3,)),
         ],
         compiler_params=pltpu.CompilerParams(vmem_limit_bytes=24 << 20),
@@ -108,18 +111,6 @@
         ),
         name="pack",
     )(*in_hbm(features, lists, hub))
-
-
-def flatten_lanes(values):
-    k, n = values.shape
-    per = 256 // k
-    lane = lax.broadcasted_iota(I32, (k, 256), 1)
-    own = lax.broadcasted_iota(I32, (k, 256), 0) == (lane & (k - 1))
-    tiled = dot(values.astype(BF16), jnp.where(own, F32(1), F32(0)).astype(BF16), TN)
-    shape = (n // per, per, 256)
-    shift = k.bit_length() - 1
-    mine = (lax.broadcasted_iota(I32, shape, 2) >> shift) == lax.broadcasted_iota(I32, shape, 1)
-    return jnp.sum(jnp.where(mine, tiled.reshape(shape), F32(0)), axis=1)
 
 
 CHUNK = 512
@@ -272,7 +263,7 @@
     ]
     get = []
     for step in range(STEPS):
-        at = pl.ds(step * STEP, STEP)
+        at = pl.ds(CUTS[step], CUTS[step + 1] - CUTS[step])
         late = min(step, 1)
         get.append(
             [
@@ -295,7 +286,7 @@
         jnp.concatenate(
             [
                 jnp.broadcast_to(inverse[:, part : part + 1], (128, 256))
-                for part in range(step * STEP // 128, (step + 1) * STEP // 128)
+                for part in range(CUTS[step] // 128, CUTS[step + 1] // 128)
             ],
             axis=0,
         )
@@ -305,14 +296,14 @@
     def gather(step):
         for copy in get[step]:
             copy.wait()
-        at = slice(step * STEP, (step + 1) * STEP)
+        at = slice(CUTS[step], CUTS[step + 1])
         total = summed[at, :]
         for hi in range(REMOTE):
             total = total + dot(table[hi, at, :].astype(BF16), remote[hi * 256 : (hi + 1) * 256])
         return (total * scales[step]).astype(BF16)
 
     def update(step, block_mean):
-        at = slice(step * STEP, (step + 1) * STEP)
+        at = slice(CUTS[step], CUTS[step + 1])
         mean[at, :] = block_mean
         pre = dot(features[at, :], self_weight[...]) + dot(block_mean, neighbour_weight[...])
         sigmoid = 0.5 * jnp.tanh(0.5 * pre) + 0.5
@@ -321,27 +312,30 @@
         block_grad = (cotangent[at, :].astype(F32) * slope).astype(BF16)
         grad_pre[at, :] = block_grad
         edge[at, :] = (dot(block_grad, neighbour_weight[...], NT) * scales[step]).astype(BF16)
+        for part, left in ((0, features[at, :]), (1, block_mean)):
+            product = dot(left, block_grad, TN)
+            for half in range(2):
+                where = (half, slice(part * WIDTH, (part + 1) * WIDTH))
+                piece = product[:, half * 128 : (half + 1) * 128]
+                weights[where] = piece if step == 0 else weights[where] + piece
 
     now = gather(0)
     for step in range(STEPS):
         later = gather(step + 1) if step + 1 < STEPS else None
         update(step, now)
         now = later
-    put = [
-        start(activations, activations_hbm, out_sems.at[0]),
-        start(grad_pre, grad_pre_hbm, out_sems.at[1]),
-        start(edge, edge_hbm, out_sems.at[2]),
-    ]
-    for part, left in ((0, features), (1, mean)):
-        product = dot(left[...], grad_pre[...], TN)
-        weights[0, part * WIDTH : (part + 1) * WIDTH, :] = product[:, :128]
-        weights[1, part * WIDTH : (part + 1) * WIDTH, :] = product[:, 128:]
+    put = []
     for half in range(2):
         for row in range(4):
             parts[pl.ds(half * 4 + row, PEERS, stride=8), :] = weights[
                 half, pl.ds(row, PEERS, stride=4), :
             ]
     message[:, 32:40, :] = parts[...].reshape(PEERS, 8, 128).astype(BF16)
+    put = [
+        start(activations, activations_hbm, out_sems.at[0], 1),
+        start(grad_pre, grad_pre_hbm, out_sems.at[1], 1),
+        start(edge, edge_hbm, out_sems.at[2], 1),
+    ]
     for hi in range(REMOTE):
         added = dot(table[hi].astype(BF16), edge[...], TN).astype(BF16).reshape(16, 16, WIDTH)
         message[hi * 16 : (hi + 1) * 16, 0:16, :] = added[:, :, :128]

time: 79.7 us -> 78.6 us (0.986)
  Pallas kernels: 37.8 us -> 36.7 us
  transfers between devices with their start and end apart: 2 -> 2, of which waited for: 2 -> 2; matrix products, arithmetic and copies ran while one was open for 0% -> 0% of each run, Pallas kernels for 21% -> 22%
where the time goes in v4:
time: 78.6 us; the launch traced here: 78.3 us
  Pallas kernels  36.7 us (47%)
  waiting for transfers between devices  24.6 us (31%)
  starting transfers between devices  16.1 us (20%)
  between operations  0.84 us (1%)
    all_to_all x1, waiting for transfers between devices, body(): lax.all_to_all(message, 'dom', split_axis=0, concat_axis=0, tiled=True)  14.6 us
    all_to_all x1, starting transfers between devices, body(): lax.all_to_all(packed, 'dom', split_axis=0, concat_axis=0, tiled=True)  11.5 us
    pallas_call x1, Pallas kernels, node(): pl.pallas_call(node_kernel, out_shape=(pltpu.HBM((NODES, WIDTH), BF16), p...  11.3 us
    all_to_all x1, waiting for transfers between devices, body(): lax.all_to_all(packed, 'dom', split_axis=0, concat_axis=0, tiled=True)  10 us
    pallas_call x1, Pallas kernels, count(): pl.pallas_call(count_kernel, out_shape=(pltpu.HBM((LOCAL + REMOTE, NODES,...  9.25 us
    pallas_call x1, Pallas kernels, local(): pl.pallas_call(local_kernel, out_shape=(pltpu.HBM((NODES, WIDTH), F32), p...  7.63 us
    pallas_call x1, Pallas kernels, finish(): pl.pallas_call(finish_kernel, out_shape=(pltpu.HBM((NODES, WIDTH), F32),...  4.63 us
    all_to_all x1, starting transfers between devices, body(): lax.all_to_all(message, 'dom', split_axis=0, concat_axis=0, tiled=True)  4.61 us
  transfers between devices with their start and end apart: 2, of which 2 were waited for; matrix products, arithmetic and copies ran while one was open for 0% of the time, Pallas kernels for 22%

profile of v4, /device:TPU:1, one launch (start us, length us, event | category | flops | bytes accessed | tf_op | source)
XLA Modules:
  0.0 78.3 jit_solution(377590300134463591)
XLA Ops:
  0.6 3.9 %pack.1 = bf16[128,16,256]{2,1,0:T(8,128)(2,1)} custom-call(bf16[2048,256]{1,0:T(8,128)(2,1)} %features_hbm.5, s32[8,128]{1,0:T(8,128)} %bitcast.6, s32[1,8]{1,0:T(1,128)} %hub_hbm.3), custom_call_target="tpu_custom_call" | custom-call | flops 1090519040 | bytes 2097152 | tf_op jit(solution)/shard_map/pack/pallas_call | solution.py:97
  4.6 11.5 %all-to-all-start = ((bf16[128,16,256]{2,1,0:T(8,128)(2,1)}), bf16[128,16,256]{2,1,0:T(8,128)(2,1)S(1)}, u32[]{:S(2)}, u32[]{:S(2)}) async-start(bf16[128,16,256]{2,1,0:T(8,128)(2,1)} %pack.1), calls=%async_computation | async-start | bytes 2097152 | tf_op jit(solution)/shard_map/all_to_all | solution.py:551
  16.1 9.2 %count.1 = (f8e4m3fn[16,2048,256]{2,1,0:T(32,128)(4,1)}, f32[2048,256]{1,0:T(8,128)}) custom-call(s32[16,2048]{1,0:T(8,128)} %bitcast.8, s32[1,2048]{1,0:T(1,128)} %bitcast.9, bf16[2048,256]{1,0:T(8,128)(2,1)} %features_hbm.5), custom_call_target="tpu_custom_call" | custom-call | flops 8589934592 | bytes 20971520 | tf_op jit(solution)/shard_map/count/pallas_call | solution.py:199
  25.3 10.0 %all-to-all-done.arrived = bf16[128,16,256]{2,1,0:T(8,128)(2,1)S(1)} async-done(((bf16[128,16,256]{2,1,0:T(8,128)(2,1)}), bf16[128,16,256]{2,1,0:T(8,128)(2,1)S(1)}, u32[]{:S(2)}, u32[]{:S(2)}) %all-to-all-start) | async-done | bytes 1048608 | tf_op jit(solution)/shard_map/all_to_all | solution.py:551
  35.4 11.3 %node.1 = (bf16[2048,256]{1,0:T(8,128)(2,1)}, bf16[2048,256]{1,0:T(8,128)(2,1)}, bf16[2048,256]{1,0:T(8,128)(2,1)}, bf16[128,40,128]{2,1,0:T(8,128)(2,1)}) custom-call(bf16[128,16,256]{2,1,0:T(8,128)(2,1)S(1)} %all-to-all-done.arrived, f8e4m3fn[16,2048,256]{2,1,0:T(32,128)(4,1)} %get-tuple-element.13.table_hbm, f32[2048,256]{1,0:T(8,128)} %get-tuple-element.14.summed_hbm, ...), custom_call_target="tpu_custom_call" | custom-call | flops 4294967296 | bytes 16777216 | tf_op jit(solution)/shard_map/node/pallas_call | solution.py:354
  46.6 4.6 %all-to-all-start.1 = ((bf16[128,40,128]{2,1,0:T(8,128)(2,1)}), bf16[128,40,128]{2,1,0:T(8,128)(2,1)S(1)}, u32[]{:S(2)}, u32[]{:S(2)}) async-start(bf16[128,40,128]{2,1,0:T(8,128)(2,1)} %get-tuple-element.16), calls=%async_computation.1 | async-start | bytes 2621440 | tf_op jit(solution)/shard_map/all_to_all | solution.py:563
  51.3 7.6 %local.1 = (f32[2048,256]{1,0:T(8,128)}, f32[4,256]{1,0:T(4,128)}) custom-call(f8e4m3fn[16,2048,256]{2,1,0:T(32,128)(4,1)} %get-tuple-element.13.table_hbm, bf16[2048,256]{1,0:T(8,128)(2,1)} %get-tuple-element.17.edge_hbm, bf16[2048,256]{1,0:T(8,128)(2,1)} %get-tuple-element.18.grad_pre_hbm, bf16[256,256]{1,0:T(8,128)(2,1)} %self_weight_hbm.3, s32[8,128]{1,0:T(8,128)} %bitcast.7), custom_call_target="tpu_custom_call" | custom-call | flops 2147483648 | bytes 14680064 | tf_op jit(solution)/shard_map/local/pallas_call | solution.py:436
  58.9 14.6 %all-to-all-done.1.returned = bf16[128,40,128]{2,1,0:T(8,128)(2,1)S(1)} async-done(((bf16[128,40,128]{2,1,0:T(8,128)(2,1)}), bf16[128,40,128]{2,1,0:T(8,128)(2,1)S(1)}, u32[]{:S(2)}, u32[]{:S(2)}) %all-to-all-start.1) | async-done | bytes 1310752 | tf_op jit(solution)/shard_map/all_to_all | solution.py:563
  73.5 4.6 %finish.1 = (f32[2048,256]{1,0:T(8,128)}, f32[4,256]{1,0:T(4,128)}) custom-call(bf16[128,40,128]{2,1,0:T(8,128)(2,1)S(1)} %all-to-all-done.1.returned, f32[2048,256]{1,0:T(8,128)} %get-tuple-element.19.grads_hbm, f32[4,256]{1,0:T(4,128)} %get-tuple-element.20.ids_hbm, s32[1,8]{1,0:T(1,128)} %hub_hbm.3), custom_call_target="tpu_custom_call" | custom-call | flops 1073741824 | bytes 6291456 | tf_op jit(solution)/shard_map/finish/pallas_call | solution.py:522
Async XLA Ops:
  4.6 30.8 %all-to-all-start = ((bf16[128,16,256]{2,1,0:T(8,128)(2,1)}), bf16[128,16,256]{2,1,0:T(8,128)(2,1)S(1)}, u32[]{:S(2)}, u32[]{:S(2)}) async-start(bf16[128,16,256]{2,1,0:T(8,128)(2,1)} %pack.1), calls=%async_computation | async-start | bytes 2097152 | tf_op jit(solution)/shard_map/all_to_all | solution.py:551
  46.6 26.8 %all-to-all-start.1 = ((bf16[128,40,128]{2,1,0:T(8,128)(2,1)}), bf16[128,40,128]{2,1,0:T(8,128)(2,1)S(1)}, u32[]{:S(2)}, u32[]{:S(2)}) async-start(bf16[128,40,128]{2,1,0:T(8,128)(2,1)} %get-tuple-element.16), calls=%async_computation.1 | async-start | bytes 2621440 | tf_op jit(solution)/shard_map/all_to_all | solution.py:563

commit v5 on v4

--- a/solution.py
+++ b/solution.py
@@ -27,7 +27,7 @@
 MESSAGE = 40
 CUTS = (0, 256, 768, 1280, 2048)
 STEPS = len(CUTS) - 1
-PIECE = 4
+PIECES = {3: (0, 4), 6: (4, 7), 7: (7, 8)}
 FINISH_PIECE = 2
 NN = (((1,), (0,)), ((), ()))
 NT = (((1,), (1,)), ((), ()))
@@ -225,7 +225,7 @@
 
 
 def node_kernel(
-    arrived,
+    arrived_hbm,
     table_hbm,
     summed_hbm,
     features_hbm,
@@ -237,6 +237,7 @@
     grad_pre_hbm,
     edge_hbm,
     message_hbm,
+    arrived,
     table,
     summed,
     features,
@@ -257,6 +258,7 @@
     message_sems,
 ):
     get_small = [
+        start(arrived_hbm, arrived, small_sems.at[3]),
         start(counts_hbm, counts, small_sems.at[0]),
         start(self_weight_hbm, self_weight, small_sems.at[1]),
         start(neighbour_weight_hbm, neighbour_weight, small_sems.at[2]),
@@ -340,8 +342,9 @@
         added = dot(table[hi].astype(BF16), edge[...], TN).astype(BF16).reshape(16, 16, WIDTH)
         message[hi * 16 : (hi + 1) * 16, 0:16, :] = added[:, :, :128]
         message[hi * 16 : (hi + 1) * 16, 16:32, :] = added[:, :, 128:]
-        if (hi + 1) % PIECE == 0:
-            peers = pl.ds((hi + 1 - PIECE) * 16, PIECE * 16)
+        if hi in PIECES:
+            first, last = PIECES[hi]
+            peers = pl.ds(first * 16, (last - first) * 16)
             put.append(start(message.at[peers], message_hbm.at[peers], message_sems.at[hi]))
     for copy in put:
         copy.wait()
@@ -359,9 +362,10 @@
             pltpu.HBM((NODES, WIDTH), BF16),
             pltpu.HBM((PEERS, MESSAGE, 128), BF16),
         ),
-        in_specs=[VMEM] + [HBM] * 7,
+        in_specs=[HBM] * 8,
         out_specs=[HBM] * 4,
         scratch_shapes=[
+            pltpu.VMEM((PEERS, SLOTS, WIDTH), BF16),
             pltpu.VMEM((REMOTE, NODES, WIDTH), COUNT),
             pltpu.VMEM((NODES, WIDTH), F32),
             rows,
@@ -376,7 +380,7 @@
             pltpu.VMEM((PEERS, MESSAGE, 128), BF16),
             pltpu.VMEM((2, 2 * WIDTH, 128), F32),
             pltpu.VMEM((8 * PEERS, 128), F32),
-            DMA((3,)),
+            DMA((4,)),
             DMA((4, STEPS)),
             DMA((3,)),
             DMA((REMOTE,)),
@@ -387,8 +391,16 @@
         ),
         name="node",
     )(
-        arrived,
-        *in_hbm(table, summed, features, counts, cotangent, self_weight, neighbour_weight),
+        *in_hbm(
+            arrived,
+            table,
+            summed,
+            features,
+            counts,
+            cotangent,
+            self_weight,
+            neighbour_weight,
+        )
     )
 
 

time: 78.6 us -> 79.9 us (1.017)
  local copies, waits for them, and re-layouts: 0 us -> 1.06 us
    unnamed x0 -> x2, local copies, waits for them, and re-layouts: none -> 1.06 us
  transfers between devices with their start and end apart: 2 -> 2, of which waited for: 2 -> 2; matrix products, arithmetic and copies ran while one was open for 0% -> 0% of each run, Pallas kernels for 22% -> 21%
where the time goes in v5:
time: 79.9 us; the launch traced here: 79.5 us
  Pallas kernels  36.9 us (46%)
  waiting for transfers between devices  24.6 us (31%)
  starting transfers between devices  16.1 us (20%)
  local copies, waits for them, and re-layouts  1.06 us (1%)
  between operations  0.84 us (1%)
    all_to_all x1, waiting for transfers between devices, body(): lax.all_to_all(message, 'dom', split_axis=0, concat_axis=0, tiled=True)  14.6 us
    all_to_all x1, starting transfers between devices, body(): lax.all_to_all(packed, 'dom', split_axis=0, concat_axis=0, tiled=True)  11.5 us
    pallas_call x1, Pallas kernels, node(): pl.pallas_call(node_kernel, out_shape=(pltpu.HBM((NODES, WIDTH), BF16), p...  11.5 us
    all_to_all x1, waiting for transfers between devices, body(): lax.all_to_all(packed, 'dom', split_axis=0, concat_axis=0, tiled=True)  10 us
    pallas_call x1, Pallas kernels, count(): pl.pallas_call(count_kernel, out_shape=(pltpu.HBM((LOCAL + REMOTE, NODES,...  9.25 us
    pallas_call x1, Pallas kernels, local(): pl.pallas_call(local_kernel, out_shape=(pltpu.HBM((NODES, WIDTH), F32), p...  7.65 us
    pallas_call x1, Pallas kernels, finish(): pl.pallas_call(finish_kernel, out_shape=(pltpu.HBM((NODES, WIDTH), F32),...  4.62 us
    all_to_all x1, starting transfers between devices, body(): lax.all_to_all(message, 'dom', split_axis=0, concat_axis=0, tiled=True)  4.61 us
  transfers between devices with their start and end apart: 2, of which 2 were waited for; matrix products, arithmetic and copies ran while one was open for 0% of the time, Pallas kernels for 21%

profile of v5, /device:TPU:1, one launch (start us, length us, event | category | flops | bytes accessed | tf_op | source)
XLA Modules:
  0.0 79.5 jit_solution(8614416487822733832)
XLA Ops:
  0.6 3.9 %pack.1 = bf16[128,16,256]{2,1,0:T(8,128)(2,1)} custom-call(bf16[2048,256]{1,0:T(8,128)(2,1)} %features_hbm.5, s32[8,128]{1,0:T(8,128)} %bitcast.6, s32[1,8]{1,0:T(1,128)} %hub_hbm.3), custom_call_target="tpu_custom_call" | custom-call | flops 1090519040 | bytes 2097152 | tf_op jit(solution)/shard_map/pack/pallas_call | solution.py:97
  4.6 11.5 %all-to-all-start = ((bf16[128,16,256]{2,1,0:T(8,128)(2,1)}), bf16[128,16,256]{2,1,0:T(8,128)(2,1)S(1)}, u32[]{:S(2)}, u32[]{:S(2)}) async-start(bf16[128,16,256]{2,1,0:T(8,128)(2,1)} %pack.1), calls=%async_computation | async-start | bytes 2097152 | tf_op jit(solution)/shard_map/all_to_all | solution.py:563
  16.1 9.2 %count.1 = (f8e4m3fn[16,2048,256]{2,1,0:T(32,128)(4,1)}, f32[2048,256]{1,0:T(8,128)}) custom-call(s32[16,2048]{1,0:T(8,128)} %bitcast.8, s32[1,2048]{1,0:T(1,128)} %bitcast.9, bf16[2048,256]{1,0:T(8,128)(2,1)} %features_hbm.5), custom_call_target="tpu_custom_call" | custom-call | flops 8589934592 | bytes 20971520 | tf_op jit(solution)/shard_map/count/pallas_call | solution.py:199
  25.3 10.0 %all-to-all-done.arrived_hbm = bf16[128,16,256]{2,1,0:T(8,128)(2,1)S(1)} async-done(((bf16[128,16,256]{2,1,0:T(8,128)(2,1)}), bf16[128,16,256]{2,1,0:T(8,128)(2,1)S(1)}, u32[]{:S(2)}, u32[]{:S(2)}) %all-to-all-start) | async-done | bytes 1048608 | tf_op jit(solution)/shard_map/all_to_all | solution.py:563
  35.4 0.0 copy-start
  35.4 1.1 %copy-done = bf16[128,16,256]{2,1,0:T(8,128)(2,1)} copy-done((bf16[128,16,256]{2,1,0:T(8,128)(2,1)}, bf16[128,16,256]{2,1,0:T(8,128)(2,1)S(1)}, u32[]{:S(2)}) %copy-start) | copy-done | bytes 1048600
  36.4 11.5 %node.1 = (bf16[2048,256]{1,0:T(8,128)(2,1)}, bf16[2048,256]{1,0:T(8,128)(2,1)}, bf16[2048,256]{1,0:T(8,128)(2,1)}, bf16[128,40,128]{2,1,0:T(8,128)(2,1)}) custom-call(bf16[128,16,256]{2,1,0:T(8,128)(2,1)} %copy-done, f8e4m3fn[16,2048,256]{2,1,0:T(32,128)(4,1)} %get-tuple-element.13.table_hbm, f32[2048,256]{1,0:T(8,128)} %get-tuple-element.14.summed_hbm, ...), custom_call_target="tpu_custom_call" | custom-call | flops 4294967296 | bytes 16777216 | tf_op jit(solution)/shard_map/node/pallas_call | solution.py:357
  47.9 4.6 %all-to-all-start.1 = ((bf16[128,40,128]{2,1,0:T(8,128)(2,1)}), bf16[128,40,128]{2,1,0:T(8,128)(2,1)S(1)}, u32[]{:S(2)}, u32[]{:S(2)}) async-start(bf16[128,40,128]{2,1,0:T(8,128)(2,1)} %get-tuple-element.16), calls=%async_computation.1 | async-start | bytes 2621440 | tf_op jit(solution)/shard_map/all_to_all | solution.py:575
  52.5 7.6 %local.1 = (f32[2048,256]{1,0:T(8,128)}, f32[4,256]{1,0:T(4,128)}) custom-call(f8e4m3fn[16,2048,256]{2,1,0:T(32,128)(4,1)} %get-tuple-element.13.table_hbm, bf16[2048,256]{1,0:T(8,128)(2,1)} %get-tuple-element.17.edge_hbm, bf16[2048,256]{1,0:T(8,128)(2,1)} %get-tuple-element.18.grad_pre_hbm, bf16[256,256]{1,0:T(8,128)(2,1)} %self_weight_hbm.3, s32[8,128]{1,0:T(8,128)} %bitcast.7), custom_call_target="tpu_custom_call" | custom-call | flops 2147483648 | bytes 14680064 | tf_op jit(solution)/shard_map/local/pallas_call | solution.py:448
  60.2 14.6 %all-to-all-done.1.returned = bf16[128,40,128]{2,1,0:T(8,128)(2,1)S(1)} async-done(((bf16[128,40,128]{2,1,0:T(8,128)(2,1)}), bf16[128,40,128]{2,1,0:T(8,128)(2,1)S(1)}, u32[]{:S(2)}, u32[]{:S(2)}) %all-to-all-start.1) | async-done | bytes 1310752 | tf_op jit(solution)/shard_map/all_to_all | solution.py:575
  74.7 4.6 %finish.1 = (f32[2048,256]{1,0:T(8,128)}, f32[4,256]{1,0:T(4,128)}) custom-call(bf16[128,40,128]{2,1,0:T(8,128)(2,1)S(1)} %all-to-all-done.1.returned, f32[2048,256]{1,0:T(8,128)} %get-tuple-element.19.grads_hbm, f32[4,256]{1,0:T(4,128)} %get-tuple-element.20.ids_hbm, s32[1,8]{1,0:T(1,128)} %hub_hbm.3), custom_call_target="tpu_custom_call" | custom-call | flops 1073741824 | bytes 6291456 | tf_op jit(solution)/shard_map/finish/pallas_call | solution.py:534
Async XLA Ops:
  4.6 30.8 %all-to-all-start = ((bf16[128,16,256]{2,1,0:T(8,128)(2,1)}), bf16[128,16,256]{2,1,0:T(8,128)(2,1)S(1)}, u32[]{:S(2)}, u32[]{:S(2)}) async-start(bf16[128,16,256]{2,1,0:T(8,128)(2,1)} %pack.1), calls=%async_computation | async-start | bytes 2097152 | tf_op jit(solution)/shard_map/all_to_all | solution.py:563
  35.4 1.1 %copy-start = (bf16[128,16,256]{2,1,0:T(8,128)(2,1)}, bf16[128,16,256]{2,1,0:T(8,128)(2,1)S(1)}, u32[]{:S(2)}) copy-start(bf16[128,16,256]{2,1,0:T(8,128)(2,1)S(1)} %all-to-all-done.arrived_hbm) | copy-start | bytes 3145732
  47.9 26.8 %all-to-all-start.1 = ((bf16[128,40,128]{2,1,0:T(8,128)(2,1)}), bf16[128,40,128]{2,1,0:T(8,128)(2,1)S(1)}, u32[]{:S(2)}, u32[]{:S(2)}) async-start(bf16[128,40,128]{2,1,0:T(8,128)(2,1)} %get-tuple-element.16), calls=%async_computation.1 | async-start | bytes 2621440 | tf_op jit(solution)/shard_map/all_to_all | solution.py:575

commit v6 on v4

--- a/solution.py
+++ b/solution.py
@@ -27,7 +27,7 @@
 MESSAGE = 40
 CUTS = (0, 256, 768, 1280, 2048)
 STEPS = len(CUTS) - 1
-PIECE = 4
+PIECES = {3: (0, 4), 6: (4, 7), 7: (7, 8)}
 FINISH_PIECE = 2
 NN = (((1,), (0,)), ((), ()))
 NT = (((1,), (1,)), ((), ()))
@@ -330,7 +330,7 @@
             parts[pl.ds(half * 4 + row, PEERS, stride=8), :] = weights[
                 half, pl.ds(row, PEERS, stride=4), :
             ]
-    message[:, 32:40, :] = parts[...].reshape(PEERS, 8, 128).astype(BF16)
+    message[:, 32:40, :] = parts[: 8 * PEERS, :].reshape(PEERS, 8, 128).astype(BF16)
     put = [
         start(activations, activations_hbm, out_sems.at[0], 1),
         start(grad_pre, grad_pre_hbm, out_sems.at[1], 1),
@@ -340,8 +340,9 @@
         added = dot(table[hi].astype(BF16), edge[...], TN).astype(BF16).reshape(16, 16, WIDTH)
         message[hi * 16 : (hi + 1) * 16, 0:16, :] = added[:, :, :128]
         message[hi * 16 : (hi + 1) * 16, 16:32, :] = added[:, :, 128:]
-        if (hi + 1) % PIECE == 0:
-            peers = pl.ds((hi + 1 - PIECE) * 16, PIECE * 16)
+        if hi in PIECES:
+            first, last = PIECES[hi]
+            peers = pl.ds(first * 16, (last - first) * 16)
             put.append(start(message.at[peers], message_hbm.at[peers], message_sems.at[hi]))
     for copy in put:
         copy.wait()
@@ -374,8 +375,8 @@
             rows,
             rows,
             pltpu.VMEM((PEERS, MESSAGE, 128), BF16),
-            pltpu.VMEM((2, 2 * WIDTH, 128), F32),
-            pltpu.VMEM((8 * PEERS, 128), F32),
+            pltpu.VMEM((2, 2 * WIDTH + 8, 128), F32),
+            pltpu.VMEM((8 * PEERS + 8, 128), F32),
             DMA((3,)),
             DMA((4, STEPS)),
             DMA((3,)),
@@ -487,7 +488,6 @@
     grad_weights[...] = jnp.concatenate([weights[:4], weights[4:]], axis=1)
     get_ids.wait()
     get_hub.wait()
-    get_grads.wait()
     put = []
     rows = lax.broadcasted_iota(I32, (BLOCK, 256), 0).astype(F32).astype(BF16)
     twice = jnp.concatenate([hub[...], hub[...]], axis=1)
@@ -510,7 +510,10 @@
         hub_hot = one_hot(
             jnp.broadcast_to(twice - block * BLOCK, (BLOCK, 16)), (BLOCK, 16), 0
         )
-        totals[at, :] = grads[at, :] + dot(hot, bound) + dot(hub_hot, hubs)
+        added = dot(hot, bound) + dot(hub_hot, hubs)
+        if block == 0:
+            get_grads.wait()
+        totals[at, :] = grads[at, :] + added
         if (block + 1) % FINISH_PIECE == 0:
             piece = pl.ds((block + 1 - FINISH_PIECE) * BLOCK, FINISH_PIECE * BLOCK)
             put.append(start(totals.at[piece], grad_features_hbm.at[piece], put_sems.at[block]))

time: 78.6 us -> 78.5 us (level)
  no operation moved by 1% of the time
where the time goes in v6:
time: 78.5 us; the launch traced here: 78.2 us
  Pallas kernels  36.6 us (47%)
  waiting for transfers between devices  24.6 us (31%)
  starting transfers between devices  16.1 us (21%)
  between operations  0.84 us (1%)
    all_to_all x1, waiting for transfers between devices, body(): lax.all_to_all(message, 'dom', split_axis=0, concat_axis=0, tiled=True)  14.6 us
    all_to_all x1, starting transfers between devices, body(): lax.all_to_all(packed, 'dom', split_axis=0, concat_axis=0, tiled=True)  11.5 us
    pallas_call x1, Pallas kernels, node(): pl.pallas_call(node_kernel, out_shape=(pltpu.HBM((NODES, WIDTH), BF16), p...  11.1 us
    all_to_all x1, waiting for transfers between devices, body(): lax.all_to_all(packed, 'dom', split_axis=0, concat_axis=0, tiled=True)  10 us
    pallas_call x1, Pallas kernels, count(): pl.pallas_call(count_kernel, out_shape=(pltpu.HBM((LOCAL + REMOTE, NODES,...  9.25 us
    pallas_call x1, Pallas kernels, local(): pl.pallas_call(local_kernel, out_shape=(pltpu.HBM((NODES, WIDTH), F32), p...  7.64 us
    pallas_call x1, Pallas kernels, finish(): pl.pallas_call(finish_kernel, out_shape=(pltpu.HBM((NODES, WIDTH), F32),...  4.66 us
    all_to_all x1, starting transfers between devices, body(): lax.all_to_all(message, 'dom', split_axis=0, concat_axis=0, tiled=True)  4.61 us
  transfers between devices with their start and end apart: 2, of which 2 were waited for; matrix products, arithmetic and copies ran while one was open for 0% of the time, Pallas kernels for 22%

profile of v6, /device:TPU:1, one launch (start us, length us, event | category | flops | bytes accessed | tf_op | source)
XLA Modules:
  0.0 78.2 jit_solution(10192465719968980653)
XLA Ops:
  0.6 3.9 %pack.1 = bf16[128,16,256]{2,1,0:T(8,128)(2,1)} custom-call(bf16[2048,256]{1,0:T(8,128)(2,1)} %features_hbm.5, s32[8,128]{1,0:T(8,128)} %bitcast.6, s32[1,8]{1,0:T(1,128)} %hub_hbm.3), custom_call_target="tpu_custom_call" | custom-call | flops 1090519040 | bytes 2097152 | tf_op jit(solution)/shard_map/pack/pallas_call | solution.py:97
  4.6 11.5 %all-to-all-start = ((bf16[128,16,256]{2,1,0:T(8,128)(2,1)}), bf16[128,16,256]{2,1,0:T(8,128)(2,1)S(1)}, u32[]{:S(2)}, u32[]{:S(2)}) async-start(bf16[128,16,256]{2,1,0:T(8,128)(2,1)} %pack.1), calls=%async_computation | async-start | bytes 2097152 | tf_op jit(solution)/shard_map/all_to_all | solution.py:554
  16.1 9.2 %count.1 = (f8e4m3fn[16,2048,256]{2,1,0:T(32,128)(4,1)}, f32[2048,256]{1,0:T(8,128)}) custom-call(s32[16,2048]{1,0:T(8,128)} %bitcast.8, s32[1,2048]{1,0:T(1,128)} %bitcast.9, bf16[2048,256]{1,0:T(8,128)(2,1)} %features_hbm.5), custom_call_target="tpu_custom_call" | custom-call | flops 8589934592 | bytes 20971520 | tf_op jit(solution)/shard_map/count/pallas_call | solution.py:199
  25.3 10.0 %all-to-all-done.arrived = bf16[128,16,256]{2,1,0:T(8,128)(2,1)S(1)} async-done(((bf16[128,16,256]{2,1,0:T(8,128)(2,1)}), bf16[128,16,256]{2,1,0:T(8,128)(2,1)S(1)}, u32[]{:S(2)}, u32[]{:S(2)}) %all-to-all-start) | async-done | bytes 1048608 | tf_op jit(solution)/shard_map/all_to_all | solution.py:554
  35.4 11.1 %node.1 = (bf16[2048,256]{1,0:T(8,128)(2,1)}, bf16[2048,256]{1,0:T(8,128)(2,1)}, bf16[2048,256]{1,0:T(8,128)(2,1)}, bf16[128,40,128]{2,1,0:T(8,128)(2,1)}) custom-call(bf16[128,16,256]{2,1,0:T(8,128)(2,1)S(1)} %all-to-all-done.arrived, f8e4m3fn[16,2048,256]{2,1,0:T(32,128)(4,1)} %get-tuple-element.13.table_hbm, f32[2048,256]{1,0:T(8,128)} %get-tuple-element.14.summed_hbm, ...), custom_call_target="tpu_custom_call" | custom-call | flops 4294967296 | bytes 16777216 | tf_op jit(solution)/shard_map/node/pallas_call | solution.py:355
  46.5 4.6 %all-to-all-start.1 = ((bf16[128,40,128]{2,1,0:T(8,128)(2,1)}), bf16[128,40,128]{2,1,0:T(8,128)(2,1)S(1)}, u32[]{:S(2)}, u32[]{:S(2)}) async-start(bf16[128,40,128]{2,1,0:T(8,128)(2,1)} %get-tuple-element.16), calls=%async_computation.1 | async-start | bytes 2621440 | tf_op jit(solution)/shard_map/all_to_all | solution.py:566
  51.1 7.6 %local.1 = (f32[2048,256]{1,0:T(8,128)}, f32[4,256]{1,0:T(4,128)}) custom-call(f8e4m3fn[16,2048,256]{2,1,0:T(32,128)(4,1)} %get-tuple-element.13.table_hbm, bf16[2048,256]{1,0:T(8,128)(2,1)} %get-tuple-element.17.edge_hbm, bf16[2048,256]{1,0:T(8,128)(2,1)} %get-tuple-element.18.grad_pre_hbm, bf16[256,256]{1,0:T(8,128)(2,1)} %self_weight_hbm.3, s32[8,128]{1,0:T(8,128)} %bitcast.7), custom_call_target="tpu_custom_call" | custom-call | flops 2147483648 | bytes 14680064 | tf_op jit(solution)/shard_map/local/pallas_call | solution.py:437
  58.8 14.6 %all-to-all-done.1.returned = bf16[128,40,128]{2,1,0:T(8,128)(2,1)S(1)} async-done(((bf16[128,40,128]{2,1,0:T(8,128)(2,1)}), bf16[128,40,128]{2,1,0:T(8,128)(2,1)S(1)}, u32[]{:S(2)}, u32[]{:S(2)}) %all-to-all-start.1) | async-done | bytes 1310752 | tf_op jit(solution)/shard_map/all_to_all | solution.py:566
  73.3 4.7 %finish.1 = (f32[2048,256]{1,0:T(8,128)}, f32[4,256]{1,0:T(4,128)}) custom-call(bf16[128,40,128]{2,1,0:T(8,128)(2,1)S(1)} %all-to-all-done.1.returned, f32[2048,256]{1,0:T(8,128)} %get-tuple-element.19.grads_hbm, f32[4,256]{1,0:T(4,128)} %get-tuple-element.20.ids_hbm, s32[1,8]{1,0:T(1,128)} %hub_hbm.3), custom_call_target="tpu_custom_call" | custom-call | flops 1073741824 | bytes 6291456 | tf_op jit(solution)/shard_map/finish/pallas_call | solution.py:525
Async XLA Ops:
  4.6 30.8 %all-to-all-start = ((bf16[128,16,256]{2,1,0:T(8,128)(2,1)}), bf16[128,16,256]{2,1,0:T(8,128)(2,1)S(1)}, u32[]{:S(2)}, u32[]{:S(2)}) async-start(bf16[128,16,256]{2,1,0:T(8,128)(2,1)} %pack.1), calls=%async_computation | async-start | bytes 2097152 | tf_op jit(solution)/shard_map/all_to_all | solution.py:554
  46.5 26.8 %all-to-all-start.1 = ((bf16[128,40,128]{2,1,0:T(8,128)(2,1)}), bf16[128,40,128]{2,1,0:T(8,128)(2,1)S(1)}, u32[]{:S(2)}, u32[]{:S(2)}) async-start(bf16[128,40,128]{2,1,0:T(8,128)(2,1)} %get-tuple-element.16), calls=%async_computation.1 | async-start | bytes 2621440 | tf_op jit(solution)/shard_map/all_to_all | solution.py:566
